TPU v7x, 256 devices: a whole 4x4x8 slice. The times are simulated.
256 devices in a mesh: tm: 4 (over y_hi, core), shot: 64 (over x, y_lo, z).
Axes of the slice: x: 4, y: 4 (y_hi: 2, y_lo: 2; y = y_hi * 2 + y_lo), z: 8, core: 2. Of those that a mesh axis runs over, the one named last changes fastest.
Arguments:
- traces: bfloat16 [2048, 128, 4096], P('shot', None, 'tm'), may hold values from -6 to 6
- shot_pos: int32 [2048], P('shot'), may hold values from 0 to 4095
- slowness: int32 [128], replicated, may hold values from -64 to 64
Outputs:
- records: float32 [256, 2, 128, 128], P(('tm', 'shot'))
All inputs are finite; a program needn't handle non-finite values.
Results may differ from a plain program's by a relative error of at most 0.0023.
Values sent between devices are 32-bit elements; how exact they have to be, the bound alone decides.
No kernel may reach another device: no remote copies, remote signals or barrier semaphores. Data moves between devices by JAX's collectives and lax.ppermute only.
A program may use at most 128 MiB of HBM per device.

v0:
```python
import math

import jax
import jax.numpy as jnp
from jax import lax
from jax.sharding import PartitionSpec as P

F = 256
FREQ0 = 16


def slant_stack(spectrum, positions, freq_bins, slowness, total_samples):
    delay_index = slowness[:, None] * positions[None, :] % total_samples
    phase_index = freq_bins[:, None, None] * delay_index[None, :, :] % total_samples
    phase = phase_index.astype(jnp.float32) * (2.0 * math.pi / total_samples)
    phase_cosine = jnp.cos(phase)
    phase_sine = jnp.sin(phase)
    real_component = spectrum[:, 0]
    imaginary_component = spectrum[:, 1]
    highest_precision = lax.Precision.HIGHEST
    receiver_real = jnp.einsum(
        "ujo,uow->ujw", phase_cosine, real_component, precision=highest_precision
    ) + jnp.einsum("ujo,uow->ujw", phase_sine, imaginary_component, precision=highest_precision)
    receiver_imaginary = jnp.einsum(
        "ujo,uow->ujw", phase_cosine, imaginary_component, precision=highest_precision
    ) - jnp.einsum("ujo,uow->ujw", phase_sine, real_component, precision=highest_precision)
    return jnp.stack([receiver_real, receiver_imaginary], axis=1)


def body(traces, shot_pos, slowness):
    shots_here, receivers, samples_here = traces.shape
    total_samples = samples_here * lax.axis_size("tm")
    freq_here = F // lax.axis_size("tm")
    time_index = lax.axis_index("tm") * samples_here + jnp.arange(samples_here, dtype=jnp.int32)
    flat_traces = traces.reshape(shots_here * receivers, samples_here)
    freq_bins = FREQ0 + jnp.int32(0) + jnp.arange(freq_here * lax.axis_size("tm"), dtype=jnp.int32)
    phase_index = freq_bins[:, None] * time_index[None, :] % total_samples
    angle = phase_index.astype(jnp.float32) * (2.0 * math.pi / total_samples)
    coeffs = jnp.stack([jnp.cos(angle), -jnp.sin(angle)], axis=1).astype(jnp.bfloat16)
    coeffs = coeffs.reshape(freq_here * lax.axis_size("tm") * 2, samples_here)
    product = lax.dot_general(
        coeffs, flat_traces, (((1,), (1,)), ((), ())), preferred_element_type=jnp.float32
    )
    owned_spec = lax.psum_scatter(
        product.reshape(freq_here * lax.axis_size("tm"), 2, shots_here * receivers),
        "tm",
        scatter_dimension=0,
        tiled=True,
    )
    spectrum = (owned_spec * jnp.float32(1.0 / math.sqrt(total_samples))).reshape(
        freq_here, 2, shots_here, receivers
    )
    shot_count = shots_here * lax.axis_size("shot")
    shot_scale = jnp.float32(1.0 / math.sqrt(shot_count))
    first_bin = FREQ0 + lax.axis_index("tm") * freq_here
    per_device = freq_here // lax.axis_size("shot")
    freq_bins = first_bin + jnp.arange(per_device * lax.axis_size("shot"), dtype=jnp.int32)
    summed = lax.psum_scatter(
        slant_stack(spectrum, shot_pos, freq_bins, slowness, total_samples),
        "shot",
        scatter_dimension=0,
        tiled=True,
    )
    return summed * shot_scale


def solution(mesh):
    in_specs = (P("shot", None, "tm"), P("shot"), P())
    out_specs = P(("tm", "shot"), None, None, None)
    return jax.shard_map(body, mesh=mesh, in_specs=in_specs, out_specs=out_specs, check_vma=False)
```

profile of v0, /device:TPU:64, one launch (start us, length us, event | category | flops | bytes accessed | tf_op | source)
XLA Modules:
  0.0 795.8 jit_solution(16771639862790726216)
XLA Ops:
  6.5 0.0 reduce-scatter.5.cloned.1.call-start
  6.5 4.5 cosine_convert_fusion
  11.1 10.1 %fusion.6 = f32[256,2,4096]{2,0,1:T(8,128)} fusion(bf16[4096,1024,1]{1,0,2:T(8,128)(2,1)} %bitcast.36, bf16[256,1,1024]{2,0,1:T(8,128)(2,1)S(1)} %get-tuple-element.6, bf16[256,1,1024]{2,0,1:T(8,128)(2,1)S(1)} %get-tuple-element.5), kind=kOutput, calls=%fused_computation.21 | convolution fusion | flops 4295491584 | bytes 17825792 | tf_op jit(solution)/shard_map/dot_general | solution.py:41
  21.2 0.0 copy-start
  21.2 0.0 copy-start.1
  21.2 0.0 reduce-scatter.5.cloned.1.call-update
  21.2 0.6 all-reduce.3.cloned.1.call-start
  21.8 0.0 copy-done
  21.8 0.0 copy-done.1
  21.8 0.1 add_select_fusion.2
  21.9 85.5 %reduce-scatter.5.cloned.1.call-done = f32[64,2,4096]{2,0,1:T(8,128)} async-done(((f32[256,2,4096]{2,0,1:T(8,128)}), f32[64,2,4096]{2,0,1:T(8,128)}) %reduce-scatter.5.cloned.1.call-update) | async-done | bytes 2097168 | tf_op jit(solution)/shard_map/reduce_scatter | solution.py:44
  107.4 1.8 broadcast_multiply_fusion
  109.2 0.4 copy.8
  109.6 10.4 %fusion.10 = f32[64,128,128]{2,1,0:T(8,128)S(1)} fusion(f32[64,2,32,128]{3,2,0,1:T(8,128)S(1)} %bitcast.31, s32[128,32]{0,1:T(8,128)S(1)} %add_select_fusion.2, s32[64]{0:T(128)S(1)} %iota_add_fusion.2), kind=kOutput, calls=%fused_computation.28 | convolution fusion | flops 406323200 | bytes 5259776 | tf_op jit(solution)/shard_map/ujo,uow->ujw/dot_general | solution.py:21
  119.9 10.5 %fusion.11 = f32[64,128,128]{2,1,0:T(8,128)S(1)} fusion(f32[64,2,32,128]{3,2,0,1:T(8,128)S(1)} %bitcast.32, s32[128,32]{0,1:T(8,128)S(1)} %add_select_fusion.2, s32[64]{0:T(128)S(1)} %iota_add_fusion.2), kind=kOutput, calls=%fused_computation.29 | convolution fusion | flops 406323200 | bytes 5259776 | tf_op jit(solution)/shard_map/ujo,uow->ujw/dot_general | solution.py:24
  130.4 10.7 %add_bitcast_fusion = f32[64,1,128,128]{3,2,0,1:T(8,128)S(1)} fusion(f32[64,128,128]{2,1,0:T(8,128)S(1)} %fusion.10, f32[64,2,32,128]{3,2,0,1:T(8,128)S(1)} %bitcast.33, s32[128,32]{0,1:T(8,128)S(1)} %add_select_fusion.2, s32[64]{0:T(128)S(1)} %iota_add_fusion.2), kind=kOutput, calls=%fused_computation.2 | convolution fusion | flops 407371776 | bytes 9454080 | tf_op jit(solution)/shard_map/ujo,uow->ujw/dot_general | solution.py:23
  141.2 10.8 %subtract_bitcast_fusion = f32[64,1,128,128]{3,2,0,1:T(8,128)S(1)} fusion(f32[64,128,128]{2,1,0:T(8,128)S(1)} %fusion.11, f32[64,2,32,128]{3,2,0,1:T(8,128)S(1)} %bitcast.34, s32[128,32]{0,1:T(8,128)S(1)} %add_select_fusion.2, s32[64]{0:T(128)S(1)} %iota_add_fusion.2), kind=kOutput, calls=%fused_computation.1 | convolution fusion | flops 407371776 | bytes 9454080 | tf_op jit(solution)/shard_map/ujo,uow->ujw/dot_general | solution.py:26
  151.9 3.8 pad_maximum_fusion
  155.7 0.0 copy-start.2
  155.7 0.0 all-reduce.3.cloned.1.call-update
  155.8 0.6 copy-done.2
  156.4 0.6 dynamic-slice
  157.0 629.5 %all-reduce.3.cloned.1.call-done = f32[64,2,128,128]{3,2,0,1:T(8,128)} async-done(((f32[64,2,128,128]{3,2,0,1:T(8,128)}), f32[64,2,128,128]{3,2,0,1:T(8,128)}) %all-reduce.3.cloned.1.call-update) | async-done | bytes 8388624
  786.5 2.2 fusion.18
  (3 shorter events, 0.0 us)
Async XLA Ops:
  6.5 100.9 %reduce-scatter.5.cloned.1.call-start = ((), (), s32[]{:S(2)}) async-start(), calls=%async_computation.1 | async-start | bytes 10485760 | tf_op jit(solution)/shard_map/reduce_scatter | solution.py:44
  21.2 0.7 copy-start
  21.2 0.7 copy-start.1
  21.2 765.3 %all-reduce.3.cloned.1.call-start = ((), (), s32[]{:S(2)}) async-start(), calls=%async_computation.2 | async-start | bytes 16777216
  155.7 0.7 copy-start.2
Sparse Core Ops, SparseCore 0:
  21.3 86.0 reduce-scatter.4
  155.9 630.5 all-reduce.2
where the time goes:
time: 801 us; the launch traced here: 796 us
  waiting for transfers between devices  715 us (89%)
  matrix products  52.5 us (7%)
  between operations  13.7 us (2%)
  other arithmetic  12.3 us (2%)
    unnamed x3, waiting for transfers between devices  630 us
    reduce_scatter x1, waiting for transfers between devices, body(): lax.psum_scatter(product.reshape(freq_here * lax.axis_size('tm'), 2, shot...  85.5 us
  transfers between devices with their start and end apart: 2, of which 2 were waited for; matrix products, arithmetic and copies ran while one was open for 0% of the time, Pallas kernels for 0%

commit v1 on v0

v1 whole, which is shorter than its diff:
```python
import math

import jax
import jax.numpy as jnp
import numpy as np
from jax import lax
from jax.experimental import pallas as pl
from jax.experimental.pallas import tpu as pltpu
from jax.sharding import Mesh, PartitionSpec as P

NT = 4096
REC = 128
F = 256
NP = 128
FREQ0 = 16
S_DEV = 32
T_DEV = 1024
SHOTS = 2048
FINE = ("yh", "c", "x", "yl", "zh", "zl")
SIZES = (2, 2, 4, 2, 4, 2)
GROUP = ("yh", "x", "yl", "zl")
N_GROUP = 32
N_SRC = 16
N_ZH = 4
VMEM = 60 * 1024 * 1024


def dft_tables():
    yh, x, yl, zl, zh = np.meshgrid(*(np.arange(n) for n in (2, 4, 2, 2, 4)), indexing="ij")
    base = (yh * 128 + x * 16 + yl * 8 + zh * 2 + zl).reshape(-1)
    out = np.empty((2, 2, 2, 128, 2, T_DEV), np.float64)
    for y in range(2):
        for c in range(2):
            t = (y * 2 + c) * T_DEV + np.arange(T_DEV)
            for half in range(2):
                k = FREQ0 + base + 64 * (c ^ half)
                angle = (k[:, None] * t[None, :] % NT) * (2.0 * math.pi / NT)
                out[y, c, half, :, 0] = np.cos(angle)
                out[y, c, half, :, 1] = -np.sin(angle)
    return out.reshape(4, 2, 256, T_DEV).astype(np.float32).astype(jnp.bfloat16)


def dft_body(table, traces, out):
    block = traces[...]
    rows = block.shape[0]
    res = lax.dot_general(
        table[...], block.reshape(rows * REC, T_DEV), (((1,), (1,)), ((), ())), preferred_element_type=jnp.float32
    )
    for s in range(rows):
        out[:, s] = res[:, s * REC : (s + 1) * REC].reshape(N_GROUP, 8, REC)


def dft_add_body(table, traces, other, out):
    block = traces[...]
    rows = block.shape[0]
    res = lax.dot_general(
        table[...], block.reshape(rows * REC, T_DEV), (((1,), (1,)), ((), ())), preferred_element_type=jnp.float32
    )
    for s in range(rows):
        out[:, s] = res[:, s * REC : (s + 1) * REC].reshape(N_GROUP, 8, REC) + other[:, s]


def dft(table, traces, other=None):
    step = 4
    spec = pl.BlockSpec((N_GROUP, step, 8, REC), lambda i: (0, i, 0, 0))
    in_specs = [
        pl.BlockSpec((256, T_DEV), lambda i: (0, 0)),
        pl.BlockSpec((step, REC, T_DEV), lambda i: (i, 0, 0)),
    ]
    args = [table, traces]
    if other is not None:
        in_specs.append(spec)
        args.append(other)
    return pl.pallas_call(
        dft_body if other is None else dft_add_body,
        grid=(S_DEV // step,),
        in_specs=in_specs,
        out_specs=spec,
        out_shape=jax.ShapeDtypeStruct((N_GROUP, S_DEV, 8, REC), jnp.float32),
        compiler_params=pltpu.CompilerParams(vmem_limit_bytes=VMEM),
        cost_estimate=pl.CostEstimate(flops=2 * 256 * 4096 * 1024, bytes_accessed=12 << 20, transcendentals=0),
        name="dft",
    )(*args)


def split(value):
    high = value.astype(jnp.bfloat16)
    return high, (value - high.astype(jnp.float32)).astype(jnp.bfloat16)


def phase_body(first, slowness, positions, high, low):
    delay = (slowness[...] * positions[...]) & (NT - 1)
    for j in range(N_ZH):
        index = ((first[0] + 2 * j) * delay) & (NT - 1)
        quadrant = (index + NT // 8) >> 10
        u = (index - (quadrant << 10)).astype(jnp.float32) * (2.0 * math.pi / NT)
        v = u * u
        sine = u + u * v * (-1.0 / 6 + v * (1.0 / 120 + v * (-1.0 / 5040 + v * (1.0 / 362880))))
        cosine = 1.0 + v * (-0.5 + v * (1.0 / 24 + v * (-1.0 / 720 + v * (1.0 / 40320 + v * (-1.0 / 3628800)))))
        odd = (quadrant & 1) == 1
        c = jnp.where(odd, sine, cosine)
        s = jnp.where(odd, cosine, sine)
        c = jnp.where(((quadrant + 1) & 2) == 2, -c, c)
        s = jnp.where((quadrant & 2) == 2, -s, s)
        high[j, :NP], low[j, :NP] = split(c)
        high[j, NP:], low[j, NP:] = split(s)


def phase_tables(first, slowness, positions):
    shape = jax.ShapeDtypeStruct((N_ZH, 2 * NP, N_SRC * S_DEV), jnp.bfloat16)
    return pl.pallas_call(
        phase_body,
        in_specs=[
            pl.BlockSpec(memory_space=pltpu.SMEM),
            pl.BlockSpec(memory_space=pltpu.VMEM),
            pl.BlockSpec(memory_space=pltpu.VMEM),
        ],
        out_specs=[pl.BlockSpec(memory_space=pltpu.VMEM)] * 2,
        out_shape=[shape, shape],
        compiler_params=pltpu.CompilerParams(vmem_limit_bytes=VMEM),
        name="phase_tables",
    )(first, slowness.reshape(NP, 1), positions.reshape(1, N_SRC * S_DEV))


def slant_body(high, low, spectra, out):
    shots = N_SRC * S_DEV
    for j in range(N_ZH):
        cols = []
        for part in range(2):
            where = pl.ds(2 * j + part, shots, stride=8)
            cols.append(spectra[0, where, :] + spectra[1, where, :])
        b_high, b_low = split(jnp.concatenate(cols, axis=1))
        a = high[j]
        dot = lambda m, n: jnp.dot(m, n, preferred_element_type=jnp.float32)
        res = dot(a, b_high) + (dot(low[j], b_high) + dot(a, b_low))
        out[j, 0] = res[:NP, :REC] + res[NP:, REC:]
        out[j, 1] = res[:NP, REC:] - res[NP:, :REC]


def slant(high, low, spectra):
    return pl.pallas_call(
        slant_body,
        in_specs=[pl.BlockSpec(memory_space=pltpu.VMEM)] * 3,
        out_specs=pl.BlockSpec(memory_space=pltpu.VMEM),
        out_shape=jax.ShapeDtypeStruct((N_ZH, 2, NP, REC), jnp.float32),
        compiler_params=pltpu.CompilerParams(vmem_limit_bytes=VMEM),
        name="slant",
    )(high, low, spectra.reshape(2, N_SRC * S_DEV * 8, REC))


def body(traces, shot_pos, slowness):
    index = {name: lax.axis_index(name) for name in FINE}
    tables = lax.dynamic_index_in_dim(jnp.asarray(dft_tables()), index["yh"] * 2 + index["c"], 0, keepdims=False)
    positions = lax.all_gather(shot_pos, ("x", "yl", "zl"), tiled=True)
    first = FREQ0 + index["yh"] * 128 + index["c"] * 64 + index["x"] * 16 + index["yl"] * 8 + index["zl"]
    high, low = phase_tables(first.reshape(1).astype(jnp.int32), slowness, positions)

    other = dft(tables[1], traces)
    other = lax.ppermute(other, "c", [(0, 1), (1, 0)])
    mine = dft(tables[0], traces, other)
    spectra = lax.all_to_all(mine, GROUP, 0, 0, tiled=True)
    partial = slant(high, low, spectra)
    partial = lax.all_to_all(partial, "zh", 0, 0, tiled=True)
    scale = jnp.float32(1.0 / math.sqrt(NT) / math.sqrt(SHOTS))
    return jnp.sum(partial, axis=0, keepdims=True) * scale


def solution(mesh):
    fine = Mesh(mesh.devices.reshape(SIZES), FINE)
    shot, tm = ("x", "yl", "zh", "zl"), ("yh", "c")
    return jax.shard_map(
        body,
        mesh=fine,
        in_specs=(P(shot, None, tm), P(shot), P()),
        out_specs=P(tm + shot, None, None, None),
        check_vma=False,
    )
```

time: 801 us -> 138 us (0.17)
  the two profiles are of different devices: /device:TPU:64 before, /device:TPU:38 now
where the time goes in v1:
time: 138 us; the launch traced here: 137 us
  blocking collectives  86.5 us (63%)
  Pallas kernels  29.2 us (21%)
  starting transfers between devices  8.67 us (6%)
  waiting for transfers between devices  7.5 us (5%)
  local copies, waits for them, and re-layouts  3.93 us (3%)
    unnamed x1, blocking collectives  67.6 us
    pallas_call x2, Pallas kernels, dft(): pl.pallas_call(dft_body if other is None else dft_add_body, grid=(S_DEV /...  19.3 us
    all_to_all x1, blocking collectives, body(): partial = lax.all_to_all(partial, 'zh', 0, 0, tiled=True)  18.8 us
    all_to_all x1, starting transfers between devices, body(): spectra = lax.all_to_all(mine, GROUP, 0, 0, tiled=True)  8.67 us
    ppermute x1, waiting for transfers between devices, body(): other = lax.ppermute(other, 'c', [(0, 1), (1, 0)])  7.5 us
    pallas_call x1, Pallas kernels, slant(): pl.pallas_call(slant_body, in_specs=[pl.BlockSpec(memory_space=pltpu.VMEM...  5.02 us
    pallas_call x1, Pallas kernels, phase_tables(): pl.pallas_call(phase_body, in_specs=[pl.BlockSpec(memory_space=pltpu.SMEM...  4.88 us
  transfers between devices with their start and end apart: 2, of which 1 were waited for; matrix products, arithmetic and copies ran while one was open for 1% of the time, Pallas kernels for 4%

profile of v1, /device:TPU:38, one launch (start us, length us, event | category | flops | bytes accessed | tf_op | source)
XLA Modules:
  0.0 137.1 jit_solution(11430446209038093011)
XLA Ops:
  0.0 2.3 %dynamic-slice_bitcast_fusion = (bf16[256,1024]{1,0:T(8,128)(2,1)}, bf16[256,1024]{1,0:T(8,128)(2,1)}) fusion(bf16[4,2,256,1024]{3,2,1,0:T(8,128)(2,1)} %constant.43.clone, s32[]{:T(128)S(6)} %select_n.4, s32[]{:T(128)S(6)} %add.31), kind=kLoop, calls=%fused_computation | loop fusion | bytes 2097160 | tf_op jit(solution)/shard_map/squeeze | solution.py:158
  2.3 9.2 %dft.2 = f32[32,32,8,128]{3,2,1,0:T(8,128)} custom-call(bf16[256,1024]{1,0:T(8,128)(2,1)} %get-tuple-element.9.table, bf16[32,128,1024]{2,1,0:T(8,128)(2,1)} %traces.3), custom_call_target="tpu_custom_call" | custom-call | flops 2147483648 | bytes 12582912 | tf_op jit(solution)/shard_map/dft/pallas_call | solution.py:74
  11.5 0.0 collective-permute-start
  11.5 7.5 %collective-permute-done.other = f32[32,32,8,128]{3,2,1,0:T(8,128)} collective-permute-done((f32[32,32,8,128]{3,2,1,0:T(8,128)}, f32[32,32,8,128]{3,2,1,0:T(8,128)}, u32[]{:S(2)}, u32[]{:S(2)}) %collective-permute-start) | collective-permute-done | bytes 4194336 | tf_op jit(solution)/shard_map/ppermute | solution.py:159
  19.0 10.1 %dft.3 = f32[32,32,8,128]{3,2,1,0:T(8,128)} custom-call(bf16[256,1024]{1,0:T(8,128)(2,1)} %get-tuple-element.10.table, bf16[32,128,1024]{2,1,0:T(8,128)(2,1)} %traces.3, f32[32,32,8,128]{3,2,1,0:T(8,128)} %collective-permute-done.other), custom_call_target="tpu_custom_call" | custom-call | flops 2147483648 | bytes 12582912 | tf_op jit(solution)/shard_map/dft/pallas_call | solution.py:74
  29.1 0.0 copy-start
  29.1 0.0 copy-start.2
  29.1 0.0 copy-start.1
  29.1 8.7 %all-to-all-start = ((f32[32,32,8,128]{3,2,1,0:T(8,128)}), f32[32,32,8,128]{3,2,1,0:T(8,128)}, u32[]{:S(2)}, u32[]{:S(2)}) async-start(f32[32,32,8,128]{3,2,1,0:T(8,128)} %dft.3), calls=%async_computation | async-start | bytes 8388608 | tf_op jit(solution)/shard_map/all_to_all | solution.py:161
  37.8 0.0 copy-done
  37.8 0.7 copy.5.slowness
  38.6 0.0 copy-done.2
  38.6 0.6 dynamic-slice
  39.8 0.0 copy-done.1
  39.8 0.2 dynamic-update-slice
  40.1 67.6 %all-reduce = s32[512]{0:T(512)} all-reduce(s32[512]{0:T(512)S(1)} %dynamic-update-slice), channel_id=1, replica_groups=mesh['yh'=2,'c'=2,'x'=4,'yl'=2,'zh'=4,'zl'=2] {'x','yl','zl'}, use_global_device_ids=true, to_apply=%add | all-reduce | flops 512 | bytes 4096
  107.7 4.9 %phase_tables.1 = (bf16[4,256,512]{2,1,0:T(8,128)(2,1)}, bf16[4,256,512]{2,1,0:T(8,128)(2,1)}) custom-call(s32[1]{0:T(128)} %bitcast.first, s32[128,1]{1,0:T(8,128)} %copy.5.slowness, s32[1,512]{1,0:T(1,128)} %bitcast.11), custom_call_target="tpu_custom_call" | custom-call | tf_op jit(solution)/shard_map/phase_tables/pallas_call | solution.py:111
  112.6 0.0 all-to-all-done
  112.6 5.0 %slant.1 = f32[4,2,128,128]{3,2,1,0:T(8,128)} custom-call(bf16[4,256,512]{2,1,0:T(8,128)(2,1)} %get-tuple-element.7.high, bf16[4,256,512]{2,1,0:T(8,128)(2,1)} %get-tuple-element.8.low, f32[2,4096,128]{2,1,0:T(8,128)} %bitcast.6.spectra), custom_call_target="tpu_custom_call" | custom-call | tf_op jit(solution)/shard_map/slant/pallas_call | solution.py:141
  117.6 18.8 %all_to_all.10 = f32[4,2,128,128]{3,2,1,0:T(8,128)S(1)} all-to-all(f32[4,2,128,128]{3,2,1,0:T(8,128)} %slant.1), channel_id=1, replica_groups=mesh['yh'=2,'c'=2,'x'=4,'yl'=2,'zh'=4,'zl'=2] {'zh'}, dimensions={0} | all-to-all | bytes 1048576 | tf_op jit(solution)/shard_map/all_to_all | solution.py:163
  136.5 0.7 multiply_bitcast_fusion
  (2 shorter events, 0.0 us)
Async XLA Ops:
  11.5 7.5 %collective-permute-start = (f32[32,32,8,128]{3,2,1,0:T(8,128)}, f32[32,32,8,128]{3,2,1,0:T(8,128)}, u32[]{:S(2)}, u32[]{:S(2)}) collective-permute-start(f32[32,32,8,128]{3,2,1,0:T(8,128)} %dft.2), channel_id=1, source_target_pairs={{0,64},{64,0},{1,65},{65,1},{2,66},{66,2},{3,67},{67,3},{4,68},{68... | collective-permute-start | bytes 12582920 | tf_op jit(solution)/shard_map/ppermute | solution.py:159
  29.1 8.7 %copy-start = (s32[128]{0:T(128)S(1)}, s32[128]{0:T(128)}, u32[]{:S(2)}) copy-start(s32[128]{0:T(128)} %param.6) | copy-start | bytes 1540
  29.1 9.4 %copy-start.2 = (u32[256]{0:T(256)S(1)}, u32[256]{0:T(256)}, u32[]{:S(2)}) copy-start(u32[256]{0:T(256)} %constant.48) | copy-start | bytes 3076
  29.1 10.7 %copy-start.1 = (s32[32]{0:T(128)S(1)}, s32[32]{0:T(128)}, u32[]{:S(2)}) copy-start(s32[32]{0:T(128)} %param.5) | copy-start | bytes 388
  29.1 83.4 %all-to-all-start = ((f32[32,32,8,128]{3,2,1,0:T(8,128)}), f32[32,32,8,128]{3,2,1,0:T(8,128)}, u32[]{:S(2)}, u32[]{:S(2)}) async-start(f32[32,32,8,128]{3,2,1,0:T(8,128)} %dft.3), calls=%async_computation | async-start | bytes 8388608 | tf_op jit(solution)/shard_map/all_to_all | solution.py:161

commit v2 on v0

v2 whole, which is shorter than its diff:
```python
import functools
import math

import jax
import jax.numpy as jnp
import numpy as np
from jax import lax
from jax.experimental import pallas as pl
from jax.experimental.pallas import tpu as pltpu
from jax.sharding import Mesh, PartitionSpec as P

NT = 4096
REC = 128
NP = 128
FREQ0 = 16
S_DEV = 32
T_DEV = 1024
SHOTS = 2048
HALF = REC // 2
PAIRS = S_DEV // 2
FINE = ("yh", "c", "x", "yl", "zh", "zl")
SIZES = (2, 2, 4, 2, 4, 2)
N_Y = 4
N_XZ = 8
N_ZH = 4
MIB = 1024 * 1024
WHOLE = pl.BlockSpec(memory_space=pltpu.VMEM)
SCALAR = pl.BlockSpec(memory_space=pltpu.SMEM)
ANY = pl.BlockSpec(memory_space=pl.ANY)


def params(flops, size, vmem=24):
    return dict(
        compiler_params=pltpu.CompilerParams(vmem_limit_bytes=vmem * MIB),
        cost_estimate=pl.CostEstimate(flops=flops, bytes_accessed=size, transcendentals=0),
    )


def dft_tables():
    d, x, zl, zh = np.meshgrid(*(np.arange(n) for n in (N_Y, 4, 2, N_ZH)), indexing="ij")
    out = np.empty((2, 2, 2, 2, 128, 2, T_DEV), np.float64)
    for yh, c, yl, half in np.ndindex(2, 2, 2, 2):
        t = (yh * 2 + c) * T_DEV + np.arange(T_DEV)
        f = (yh ^ (d >> 1)) * 128 + (c ^ half) * 64 + x * 16 + (yl ^ (d & 1)) * 8 + zh * 2 + zl
        angle = ((FREQ0 + f).reshape(-1, 1) * t % NT) * (2.0 * math.pi / NT)
        out[yh, c, yl, half, :, 0] = np.cos(angle)
        out[yh, c, yl, half, :, 1] = -np.sin(angle)
    return out.reshape(8, 2, 256, T_DEV).astype(np.float32).astype(jnp.bfloat16)


def spectra(table, traces):
    rows = traces.shape[0]
    res = lax.dot_general(
        table[0, 0], traces[...].reshape(rows * HALF, T_DEV), (((1,), (1,)), ((), ())), preferred_element_type=jnp.float32
    )
    return [res[:, s * 128 : (s + 1) * 128].reshape(N_Y, N_XZ, 8, 128) for s in range(rows // 2)]


def other_body(n_after, index, table, traces, *rest):
    out = rest[n_after]
    for s, block in enumerate(spectra(table, traces)):
        out[:, :, s] = block


def mine_a_body(n_after, index, table, traces, other, *rest):
    outs = rest[n_after:]
    for s, block in enumerate(spectra(table, traces)):
        for d, out in enumerate(outs):
            out[:, s] = block[d] + other[d, :, s]


def mine_b_body(n_after, index, table, traces, other, here, there, *rest):
    out = rest[n_after]
    step = pl.program_id(0)
    blocks = spectra(table, traces)
    for s, block in enumerate(blocks):
        for d in range(N_Y):
            out[:, d * PAIRS + step * len(blocks) + s] = block[d] + other[d, :, s]

    @pl.when(step == 0)
    def _():
        tile = jnp.concatenate([here[:2], there[:2], jnp.zeros((4, 128), jnp.float32)], axis=0)
        out[:, N_Y * PAIRS] = jnp.broadcast_to(tile, (N_XZ, 8, 128))


def dft(index, tables, traces, half, chunk, other=None, after=(), places=()):
    step = 16
    n = step // 2
    by_d = pl.BlockSpec((N_Y, N_XZ, n, 8, 128), lambda i, index: (0, 0, i, 0, 0))
    f32 = lambda *shape: jax.ShapeDtypeStruct(shape, jnp.float32)
    if other is None:
        body, out_specs, out_shape = other_body, by_d, f32(N_Y, N_XZ, PAIRS, 8, 128)
    elif chunk == 0:
        body = mine_a_body
        out_specs = [pl.BlockSpec((N_XZ, n, 8, 128), lambda i, index: (0, i, 0, 0))] * N_Y
        out_shape = [f32(N_XZ, PAIRS, 8, 128)] * N_Y
    else:
        body = mine_b_body
        out_specs = pl.BlockSpec((N_XZ, N_Y * PAIRS + 1, 8, 128), lambda i, index: (0, 0, 0, 0))
        out_shape = f32(N_XZ, N_Y * PAIRS + 1, 8, 128)
    return pl.pallas_call(
        functools.partial(body, len(after)),
        grid_spec=pltpu.PrefetchScalarGridSpec(
            num_scalar_prefetch=1,
            grid=(S_DEV // step,),
            in_specs=[
                pl.BlockSpec((1, 1, 256, T_DEV), lambda i, index: (index[0], half, 0, 0)),
                pl.BlockSpec((step, HALF, T_DEV), lambda i, index: (i, chunk, 0)),
            ]
            + ([] if other is None else [by_d])
            + [pl.BlockSpec((8, 128), lambda i, index: (0, 0))] * len(places)
            + [ANY] * len(after),
            out_specs=out_specs,
        ),
        out_shape=out_shape,
        name=("other" if other is None else "mine") + ("_a", "_b")[chunk],
        **params(2 * 256 * 2048 * 1024, 7 << 20, 50),
    )(index, tables, traces, *([] if other is None else [other]), *places, *after)


def sum_a_body(own, yl, yh, both, *rest):
    out = rest[-1]
    out[:, 0] = own[...] + yh[...]
    out[:, 1] = yl[...] + both[...]


def sum_a(parts, after=()):
    spec = pl.BlockSpec((2, PAIRS, 8, 128), lambda i: (i, 0, 0, 0))
    return pl.pallas_call(
        sum_a_body,
        grid=(N_XZ // 2,),
        in_specs=[spec] * N_Y + [ANY] * len(after),
        out_specs=pl.BlockSpec((2, 2, PAIRS, 8, 128), lambda i: (i, 0, 0, 0, 0)),
        out_shape=jax.ShapeDtypeStruct((N_XZ, 2, PAIRS, 8, 128), jnp.float32),
        name="sum_a",
        **params(1 << 18, 3 << 20),
    )(*parts, *after)


def split(value):
    high = value.astype(jnp.bfloat16)
    return high, (value - high.astype(jnp.float32)).astype(jnp.bfloat16)


def turn(index):
    index = index & (NT - 1)
    quadrant = (index + NT // 8) >> 10
    u = (index - (quadrant << 10)).astype(jnp.float32) * (2.0 * math.pi / NT)
    v = u * u
    sine = u + u * v * (-1.0 / 6 + v * (1.0 / 120 + v * (-1.0 / 5040 + v * (1.0 / 362880))))
    cosine = 1.0 + v * (-0.5 + v * (1.0 / 24 + v * (-1.0 / 720 + v * (1.0 / 40320 + v * (-1.0 / 3628800)))))
    odd = (quadrant & 1) == 1
    c = jnp.where(odd, sine, cosine)
    s = jnp.where(odd, cosine, sine)
    return jnp.where(((quadrant + 1) & 2) == 2, -c, c), jnp.where((quadrant & 2) == 2, -s, s)


def times(a, b):
    return a[0] * b[0] - a[1] * b[1], a[1] * b[0] + a[0] * b[1]


def phase_tables(n_d, base, yh, yl, slowness, positions, column, slow, high, low):
    slow[...] = jnp.broadcast_to(slowness[...].astype(jnp.float32), (NP, 128)).T.astype(jnp.int32)
    first = base[0] + yh[0] * 128 + yl[0] * 8
    rows = 16

    def step(i, _):
        row = pl.multiple_of(i * rows, rows)
        delay = (slow[pl.ds(row, rows), :] * positions) & (NT - 1)
        own = turn(first * delay)
        forms = [own]
        if n_d > 1:
            by_yl = turn((8 - 16 * yl[0]) * delay)
            by_yh = turn((128 - 256 * yh[0]) * delay)
            other = times(own, by_yh)
            forms = [own, times(own, by_yl), other, times(other, by_yl)]
        by_zh = turn(2 * delay)
        for d, value in enumerate(forms):
            for j in range(N_ZH):
                if j > 0:
                    value = times(value, by_zh)
                for k in range(2):
                    where = (d * N_ZH + j, pl.ds(k * NP + row, rows), slice(column, column + 128))
                    high[where], low[where] = split(value[k])
        return 0

    lax.fori_loop(0, NP // rows, step, 0)


def stack(high, low, real, imag):
    left = lax.broadcasted_iota(jnp.int32, real.shape, 1) < HALF
    even = jnp.where(left, real, pltpu.roll(imag, HALF, 1))
    odd = jnp.where(left, pltpu.roll(real, HALF, 1), imag)
    b_high, b_low = split(jnp.concatenate([even, odd], axis=0))
    both = jnp.dot(high, jnp.concatenate([b_high, b_low], axis=1), preferred_element_type=jnp.float32)
    res = both[:, :128] + (jnp.dot(low, b_high, preferred_element_type=jnp.float32) + both[:, 128:])
    cross = pltpu.roll(res[NP:], HALF, 1)
    left = lax.broadcasted_iota(jnp.int32, (NP, 128), 1) < HALF
    return res[:NP] + jnp.where(left, cross, -cross)


def slant_a_body(zh, base, yh, yl, slowness, places, data, *rest):
    parts, outs, (slow, high, low) = rest[:N_Y], rest[N_Y : N_Y + N_ZH], rest[N_Y + N_ZH :]
    for parity in range(2):
        for place in range(2):
            row = 2 * place + parity
            positions = places[row : row + 1, :].astype(jnp.int32)
            phase_tables(1, base, yh, yl, slowness, positions, (2 * parity + place) * 128, slow, high, low)
    for e, out in enumerate(outs):
        j = (zh[0] + e) & (N_ZH - 1)
        cols = []
        for part in range(2):
            rows = [data[:, pl.ds(place * PAIRS * 8 + 2 * j + part, PAIRS, stride=8), :] for place in range(2)]
            cols.append(jnp.concatenate([row.reshape(N_XZ * PAIRS, 128) for row in rows], axis=0))
        out[0] = stack(high[j], low[j], *cols)
        out[1] = (parts[0][j] + parts[1][j]) + (parts[2][j] + parts[3][j])


def slant_a(zh, base, yh, yl, slowness, places, data, parts):
    return pl.pallas_call(
        slant_a_body,
        in_specs=[SCALAR] * 4 + [WHOLE] * (3 + N_Y),
        out_specs=[WHOLE] * N_ZH,
        out_shape=[jax.ShapeDtypeStruct((2, NP, 128), jnp.float32)] * N_ZH,
        scratch_shapes=[pltpu.VMEM((NP, 128), jnp.int32)] + [pltpu.VMEM((N_ZH, 2 * NP, 512), jnp.bfloat16)] * 2,
        name="slant_a",
        **params(1 << 30, 5 << 20),
    )(zh, base, yh, yl, slowness, places, data.reshape(N_XZ, 2 * PAIRS * 8, 128), *parts)


def slant_b_body(n_after, base, yh, yl, slowness, data, *rest):
    rest = rest[n_after:]
    outs, here, (slow, high, low) = rest[:N_Y], rest[N_Y], rest[N_Y + 1 :]
    here[...] = jnp.sum(data[:, N_Y * PAIRS * 8 :, :], axis=0)
    for parity in range(2):
        row = here[parity : parity + 1, :].astype(jnp.int32)
        phase_tables(N_Y, base, yh, yl, slowness, row, parity * 128, slow, high, low)
    for d, out in enumerate(outs):
        for j in range(N_ZH):
            cols = [
                data[:, pl.ds(d * PAIRS * 8 + 2 * j + part, PAIRS, stride=8), :].reshape(N_XZ * PAIRS, 128)
                for part in range(2)
            ]
            out[j] = stack(high[d * N_ZH + j], low[d * N_ZH + j], *cols)


def slant_b(base, yh, yl, slowness, data, after=()):
    return pl.pallas_call(
        functools.partial(slant_b_body, len(after)),
        in_specs=[SCALAR] * 3 + [WHOLE] * 2 + [ANY] * len(after),
        out_specs=[WHOLE] * (N_Y + 1),
        out_shape=[jax.ShapeDtypeStruct((N_ZH, NP, 128), jnp.float32)] * N_Y + [jax.ShapeDtypeStruct((8, 128), jnp.float32)],
        scratch_shapes=[pltpu.VMEM((NP, 128), jnp.int32)] + [pltpu.VMEM((N_Y * N_ZH, 2 * NP, 256), jnp.bfloat16)] * 2,
        name="slant_b",
        **params(1 << 31, 7 << 20),
    )(base, yh, yl, slowness, data.reshape(N_XZ, (N_Y * PAIRS + 1) * 8, 128), *after)


def finish_body(own, *rest):
    scale = jnp.float32(1.0 / math.sqrt(NT) / math.sqrt(SHOTS))
    left = lax.broadcasted_iota(jnp.int32, (NP, 128), 1) < HALF
    out = rest[-1]
    a, b = (((own[i] + rest[0][i]) + (rest[1][i] + rest[2][i])) * scale for i in range(2))
    out[0, 0] = jnp.where(left, a, pltpu.roll(b, HALF, 1))
    out[0, 1] = jnp.where(left, pltpu.roll(a, HALF, 1), b)


def finish(parts):
    return pl.pallas_call(
        finish_body,
        in_specs=[WHOLE] * N_ZH,
        out_specs=WHOLE,
        out_shape=jax.ShapeDtypeStruct((1, 2, NP, REC), jnp.float32),
        name="finish",
        **params(1 << 18, 1 << 20),
    )(*parts)


def swap(value, axes, size, mask):
    return lax.ppermute(value, axes, [(i, i ^ mask) for i in range(size)])


def exchange_y(parts):
    return [parts[0]] + [swap(parts[d], ("yh", "yl"), N_Y, d) for d in range(1, N_Y)]


def exchange_z(parts):
    shift = lambda e: [(i, (i + e) % N_ZH) for i in range(N_ZH)]
    return [parts[0]] + [lax.ppermute(parts[e], "zh", shift(e)) for e in range(1, N_ZH)]


def body(traces, shot_pos, slowness):
    yh, c, x, yl, zh, zl = (lax.axis_index(name) for name in FINE)
    one = lambda value: value.reshape(1)

    slot = (jnp.arange(N_XZ) == x * 2 + zl).astype(jnp.int32)
    places = (shot_pos.reshape(1, PAIRS, 2) * slot[:, None, None]).reshape(N_XZ * PAIRS, 2).T
    places = jnp.pad(places.astype(jnp.float32), ((0, 6), (0, 0)))

    tables = jnp.asarray(dft_tables())
    index = one(yh * 4 + c * 2 + yl)
    other_a = dft(index, tables, traces, 1, 0)
    other_b = dft(index, tables, traces, 1, 1, after=[other_a])
    mine_a = dft(index, tables, traces, 0, 0, swap(other_a, "c", 2, 1), after=[other_b])
    there = swap(places, "yl", 2, 1)
    mine_b = dft(index, tables, traces, 0, 1, swap(other_b, "c", 2, 1), after=[mine_a[0]], places=[places, there])
    data_b = lax.all_to_all(mine_b, ("x", "zl"), 0, 0, tiled=True)

    where = one(FREQ0 + c * 64 + x * 16 + zl), one(yh), one(yl), slowness.reshape(1, NP)
    *part_b, places = slant_b(*where, data_b)
    data_a = lax.all_to_all(sum_a(exchange_y(mine_a), after=[places]), ("x", "zl"), 0, 0, tiled=True)
    return finish(exchange_z(slant_a(one(zh), *where, places, data_a, exchange_y(part_b))))


def solution(mesh):
    fine = Mesh(mesh.devices.reshape(SIZES), FINE)
    shot, tm = ("x", "yl", "zh", "zl"), ("yh", "c")
    return jax.shard_map(
        body,
        mesh=fine,
        in_specs=(P(shot, None, tm), P(shot), P()),
        out_specs=P(tm + shot, None, None, None),
        check_vma=False,
    )
```

time: 801 us -> 108 us (0.13)
  the two profiles are of different devices: /device:TPU:64 before, /device:TPU:1 now
where the time goes in v2:
time: 108 us
  waiting for transfers between devices  46.8 us (43%)
  starting transfers between devices  27.9 us (26%)
  Pallas kernels  27.3 us (25%)
  local copies, waits for them, and re-layouts  5.48 us (5%)
    all_to_all x1, waiting for transfers between devices, body(): data_b = lax.all_to_all(mine_b, ('x', 'zl'), 0, 0, tiled=True)  22.6 us
    pallas_call x4, Pallas kernels, dft(): pl.pallas_call(functools.partial(body, len(after)), grid_spec=pltpu.Prefe...  16.4 us
    ppermute x9, waiting for transfers between devices, swap(): return lax.ppermute(value, axes, [(i, i ^ mask) for i in range(size)])  13 us
    ppermute x3, waiting for transfers between devices, exchange_z(): lax.ppermute(parts[e], 'zh', shift(e))  11.2 us
    ppermute x9, starting transfers between devices, swap(): return lax.ppermute(value, axes, [(i, i ^ mask) for i in range(size)])  11.2 us
    ppermute x3, starting transfers between devices, exchange_z(): lax.ppermute(parts[e], 'zh', shift(e))  8.44 us
    unnamed x24, local copies, waits for them, and re-layouts  5.08 us
    all_to_all x1, starting transfers between devices, body(): data_b = lax.all_to_all(mine_b, ('x', 'zl'), 0, 0, tiled=True)  4.37 us
  transfers between devices with their start and end apart: 14, of which 7 were waited for; matrix products, arithmetic and copies ran while one was open for 0% of the time, Pallas kernels for 10%

profile of v2, /device:TPU:1, one launch (start us, length us, event | category | flops | bytes accessed | tf_op | source)
XLA Modules:
  0.0 107.7 jit_solution(11227662388863961300)
XLA Ops:
  0.0 4.2 %other_a.1.rest_0_ = f32[4,8,16,8,128]{4,3,2,1,0:T(8,128)} custom-call(s32[1]{0:T(128)} %bitcast.5.index, bf16[8,2,256,1024]{3,2,1,0:T(8,128)(2,1)} %constant.36.clone.table, bf16[32,128,1024]{2,1,0:T(8,128)(2,1)} %traces.7), custom_call_target="tpu_custom_call" | custom-call | flops 1073741824 | bytes 7340032 | tf_op jit(solution)/shard_map/other_a/pallas_call | solution.py:101
  4.2 0.0 copy-start.11
  4.2 3.2 %collective-permute-start.2 = (f32[4,8,16,8,128]{4,3,2,1,0:T(8,128)}, f32[4,8,16,8,128]{4,3,2,1,0:T(8,128)}, u32[]{:S(2)}, u32[]{:S(2)}) collective-permute-start(f32[4,8,16,8,128]{4,3,2,1,0:T(8,128)} %other_a.1.rest_0_), channel_id=1, source_target_pairs={{0,64},{64,0},{1,65},{65,1},{2,66},{66,2},{3,67},{67,3},{4,68},{68... | collective-permute-start | bytes 6291464 | tf_op jit(solution)/shard_map/ppermute | solution.py:280
  7.5 3.3 %other_b.1.rest_0_ = f32[4,8,16,8,128]{4,3,2,1,0:T(8,128)S(1)} custom-call(s32[1]{0:T(128)} %bitcast.5.index, bf16[8,2,256,1024]{3,2,1,0:T(8,128)(2,1)} %constant.36.clone.table, bf16[32,128,1024]{2,1,0:T(8,128)(2,1)} %traces.7, f32[4,8,16,8,128]{4,3,2,1,0:T(8,128)} %other_a.1.rest_0_), custom_call_target="tpu_custom_call" | custom-call | flops 1073741824 | bytes 7340032 | tf_op jit(solution)/shard_map/other_b/pallas_call | solution.py:101
  10.8 0.0 copy-start
  10.8 0.1 collective-permute-start
  10.9 0.1 mul.45
  11.0 0.1 mul.46
  11.1 0.0 copy-done.11
  11.1 0.1 mul.41
  11.1 0.1 copy.6
  11.2 0.1 mul.43
  11.3 0.1 collective-permute-start.1
  11.4 0.2 collective-permute-done.2.other
  11.6 0.6 copy-done
  12.2 3.8 %mine_a.1 = (f32[8,16,8,128]{3,2,1,0:T(8,128)S(1)}, f32[8,16,8,128]{3,2,1,0:T(8,128)S(1)}, f32[8,16,8,128]{3,2,1,0:T(8,128)S(1)}, f32[8,16,8,128]{3,2,1,0:T(8,128)S(1)}) custom-call(s32[1]{0:T(128)} %bitcast.5.index, bf16[8,2,256,1024]{3,2,1,0:T(8,128)(2,1)} %constant.36.clone.table, bf16[32,128,1024]{2,1,0:T(8,128)(2,1)} %traces.7, ...), custom_call_target="tpu_custom_call" | custom-call | flops 1073741824 | bytes 7340032 | tf_op jit(solution)/shard_map/mine_a/pallas_call | solution.py:101
  15.9 0.0 copy-start.1
  16.0 0.8 copy-done.1
  16.8 0.0 copy-start.2
  16.8 0.8 copy-done.2
  17.6 0.0 copy-start.3
  17.6 0.8 copy-done.3
  18.4 0.0 collective-permute-done.1.there
  18.4 0.0 collective-permute-done.other
  18.4 5.1 %mine_b.1 = f32[8,65,8,128]{3,2,1,0:T(8,128)} custom-call(s32[1]{0:T(128)} %bitcast.5.index, bf16[8,2,256,1024]{3,2,1,0:T(8,128)(2,1)} %constant.36.clone.table, bf16[32,128,1024]{2,1,0:T(8,128)(2,1)} %traces.7, f32[4,8,16,8,128]{4,3,2,1,0:T(8,128)} %collective-permute-done.other, f32[8,128]{1,0:T(8,128)S(1)} %pad.4.here, ...), custom_call_target="tpu_custom_call" | custom-call | flops 1073741824 | bytes 7340032 | tf_op jit(solution)/shard_map/mine_b/pallas_call | solution.py:101
  23.5 4.4 %all-to-all-start = ((f32[8,65,8,128]{3,2,1,0:T(8,128)}), f32[8,65,8,128]{3,2,1,0:T(8,128)S(1)}, u32[]{:S(2)}, u32[]{:S(2)}) async-start(f32[8,65,8,128]{3,2,1,0:T(8,128)} %mine_b.1), calls=%async_computation | async-start | bytes 4259840 | tf_op jit(solution)/shard_map/all_to_all | solution.py:307
  27.8 0.7 collective-permute-start.3
  28.5 2.6 %collective-permute-start.4 = (f32[8,16,8,128]{3,2,1,0:T(8,128)}, f32[8,16,8,128]{3,2,1,0:T(8,128)}, u32[]{:S(2)}, u32[]{:S(2)}) collective-permute-start(f32[8,16,8,128]{3,2,1,0:T(8,128)} %copy-done.2), channel_id=1, source_target_pairs={{0,128},{8,136},{128,0},{136,8},{1,129},{9,137},{129,1},{137,9},{2... | collective-permute-start | bytes 1572872 | tf_op jit(solution)/shard_map/ppermute | solution.py:280
  31.1 0.5 collective-permute-start.5
  31.7 22.6 %all-to-all-done = f32[8,65,8,128]{3,2,1,0:T(8,128)S(1)} async-done(((f32[8,65,8,128]{3,2,1,0:T(8,128)}), f32[8,65,8,128]{3,2,1,0:T(8,128)S(1)}, u32[]{:S(2)}, u32[]{:S(2)}) %all-to-all-start) | async-done | bytes 2129952 | tf_op jit(solution)/shard_map/all_to_all | solution.py:307
  54.2 0.0 copy-done.8
  54.3 3.8 %slant_b.1 = (f32[4,128,128]{2,1,0:T(8,128)S(1)}, f32[4,128,128]{2,1,0:T(8,128)S(1)}, f32[4,128,128]{2,1,0:T(8,128)S(1)}, f32[4,128,128]{2,1,0:T(8,128)S(1)}, f32[8,128]{1,0:T(8,128)S(1)}) custom-call(s32[1]{0:T(128)} %bitcast.1.base, s32[1]{0:T(128)} %bitcast.2.yh, s32[1]{0:T(128)} %bitcast.3.yl, s32[1,128]{1,0:T(1,128)S(1)} %bitcast.14, ...), custom_call_target="tpu_custom_call" | custom-call | flops 2147483648 | bytes 7340032 | tf_op jit(solution)/shard_map/slant_b/pallas_call | solution.py:248
  58.0 0.0 copy-start.4
  58.1 0.7 copy-done.4
  58.8 0.0 copy-start.6
  58.8 0.7 copy-done.6
  59.4 0.0 copy-start.9
  59.4 0.7 copy-done.9
  60.1 0.0 collective-permute-done.3.yl
  60.1 0.0 collective-permute-done.4.yh
  60.1 0.0 collective-permute-done.5.both
  60.1 0.0 copy-start.7
  60.2 0.0 copy-start.5
  60.2 0.0 copy-start.10
  60.2 3.5 %sum_a.1 = f32[8,2,16,8,128]{4,3,2,1,0:T(8,128)} custom-call(f32[8,16,8,128]{3,2,1,0:T(8,128)S(1)} %get-tuple-element.18.rest_0_.own, f32[8,16,8,128]{3,2,1,0:T(8,128)S(1)} %collective-permute-done.3.yl, f32[8,16,8,128]{3,2,1,0:T(8,128)} %collective-permute-done.4.yh, f32[8,16,8,128]{3,2,1,0:T(8,128)} %collective-permute-done.5.both, ...), custom_call_target="tpu_custom_call" | custom-call | flops 262144 | bytes 3145728 | tf_op jit(solution)/shard_map/sum_a/pallas_call | solution.py:129
  63.7 3.9 %all-to-all-start.1 = ((f32[8,2,16,8,128]{4,3,2,1,0:T(8,128)}), f32[8,2,16,8,128]{4,3,2,1,0:T(8,128)S(1)}, u32[]{:S(2)}, u32[]{:S(2)}) async-start(f32[8,2,16,8,128]{4,3,2,1,0:T(8,128)} %sum_a.1), calls=%async_computation.1 | async-start | bytes 2097152 | tf_op jit(solution)/shard_map/all_to_all | solution.py:311
  67.6 0.0 copy-done.7
  67.6 1.0 collective-permute-start.6
  68.6 0.0 copy-done.5
  68.6 2.4 %collective-permute-start.7 = (f32[4,128,128]{2,1,0:T(8,128)S(1)}, f32[4,128,128]{2,1,0:T(8,128)S(1)}, u32[]{:S(2)}, u32[]{:S(2)}) collective-permute-start(f32[4,128,128]{2,1,0:T(8,128)S(1)} %copy-done.5), channel_id=1, source_target_pairs={{0,128},{8,136},{128,0},{136,8},{1,129},{9,137},{129,1},{137,9},{2... | collective-permute-start | bytes 786440 | tf_op jit(solution)/shard_map/ppermute | solution.py:280
  71.0 0.5 collective-permute-start.8
  71.5 2.4 %collective-permute-done.6.rest_1_ = f32[4,128,128]{2,1,0:T(8,128)S(1)} collective-permute-done((f32[4,128,128]{2,1,0:T(8,128)S(1)}, f32[4,128,128]{2,1,0:T(8,128)S(1)}, u32[]{:S(2)}, u32[]{:S(2)}) %collective-permute-start.6) | collective-permute-done | bytes 262176 | tf_op jit(solution)/shard_map/ppermute | solution.py:280
  73.9 7.5 %collective-permute-done.7.rest_2_ = f32[4,128,128]{2,1,0:T(8,128)S(1)} collective-permute-done((f32[4,128,128]{2,1,0:T(8,128)S(1)}, f32[4,128,128]{2,1,0:T(8,128)S(1)}, u32[]{:S(2)}, u32[]{:S(2)}) %collective-permute-start.7) | collective-permute-done | bytes 262176 | tf_op jit(solution)/shard_map/ppermute | solution.py:280
  81.5 2.9 %collective-permute-done.8.rest_3_ = f32[4,128,128]{2,1,0:T(8,128)S(1)} collective-permute-done((f32[4,128,128]{2,1,0:T(8,128)S(1)}, f32[4,128,128]{2,1,0:T(8,128)S(1)}, u32[]{:S(2)}, u32[]{:S(2)}) %collective-permute-start.8) | collective-permute-done | bytes 262176 | tf_op jit(solution)/shard_map/ppermute | solution.py:280
  84.4 0.0 all-to-all-done.1
  84.4 0.0 copy-done.10
  84.4 2.9 %slant_a.1 = (f32[2,128,128]{2,1,0:T(8,128)S(1)}, f32[2,128,128]{2,1,0:T(8,128)S(1)}, f32[2,128,128]{2,1,0:T(8,128)S(1)}, f32[2,128,128]{2,1,0:T(8,128)S(1)}) custom-call(s32[1]{0:T(128)} %bitcast.zh, s32[1]{0:T(128)} %bitcast.1.base, s32[1]{0:T(128)} %bitcast.2.yh, s32[1]{0:T(128)} %bitcast.3.yl, s32[1,128]{1,0:T(1,128)S(1)} %bitcast.15, ...), custom_call_target="tpu_custom_call" | custom-call | flops 1073741824 | bytes 5242880 | tf_op jit(solution)/shard_map/slant_a/pallas_call | solution.py:220
  87.2 6.1 %collective-permute-start.10 = (f32[2,128,128]{2,1,0:T(8,128)S(1)}, f32[2,128,128]{2,1,0:T(8,128)S(1)}, u32[]{:S(2)}, u32[]{:S(2)}) collective-permute-start(f32[2,128,128]{2,1,0:T(8,128)S(1)} %get-tuple-element.29), channel_id=1, source_target_pairs={{0,4},{2,6},{4,0},{6,2},{1,5},{3,7},{5,1},{7,3},{8,12},{10,14},{12... | collective-permute-start | bytes 393224 | tf_op jit(solution)/shard_map/ppermute | solution.py:289
  93.3 0.3 collective-permute-start.11
  93.6 2.1 %collective-permute-start.9 = (f32[2,128,128]{2,1,0:T(8,128)S(1)}, f32[2,128,128]{2,1,0:T(8,128)S(1)}, u32[]{:S(2)}, u32[]{:S(2)}) collective-permute-start(f32[2,128,128]{2,1,0:T(8,128)S(1)} %get-tuple-element.28), channel_id=1, source_target_pairs={{0,2},{2,4},{4,6},{6,0},{1,3},{3,5},{5,7},{7,1},{8,10},{10,12},{12... | collective-permute-start | bytes 393224 | tf_op jit(solution)/shard_map/ppermute | solution.py:289
  95.7 0.1 collective-permute-done.10.rest_1_
  95.8 11.2 %collective-permute-done.11.rest_2_ = f32[2,128,128]{2,1,0:T(8,128)S(1)} collective-permute-done((f32[2,128,128]{2,1,0:T(8,128)S(1)}, f32[2,128,128]{2,1,0:T(8,128)S(1)}, u32[]{:S(2)}, u32[]{:S(2)}) %collective-permute-start.11) | collective-permute-done | bytes 131104 | tf_op jit(solution)/shard_map/ppermute | solution.py:289
  106.9 0.0 collective-permute-done.9.rest_0_
  106.9 0.8 finish.1
  (5 shorter events, 0.0 us)
Async XLA Ops:
  4.2 6.8 %copy-start.11 = (s32[32]{0:T(128)S(1)}, s32[32]{0:T(128)}, u32[]{:S(2)}) copy-start(s32[32]{0:T(128)} %param.5) | copy-start | bytes 388
  4.2 7.4 %collective-permute-start.2 = (f32[4,8,16,8,128]{4,3,2,1,0:T(8,128)}, f32[4,8,16,8,128]{4,3,2,1,0:T(8,128)}, u32[]{:S(2)}, u32[]{:S(2)}) collective-permute-start(f32[4,8,16,8,128]{4,3,2,1,0:T(8,128)} %other_a.1.rest_0_), channel_id=1, source_target_pairs={{0,64},{64,0},{1,65},{65,1},{2,66},{66,2},{3,67},{67,3},{4,68},{68... | collective-permute-start | bytes 6291464 | tf_op jit(solution)/shard_map/ppermute | solution.py:280
  10.8 1.4 %copy-start = (f32[4,8,16,8,128]{4,3,2,1,0:T(8,128)}, f32[4,8,16,8,128]{4,3,2,1,0:T(8,128)S(1)}, u32[]{:S(2)}) copy-start(f32[4,8,16,8,128]{4,3,2,1,0:T(8,128)S(1)} %other_b.1.rest_0_) | copy-start | bytes 6291460
  10.8 7.6 %collective-permute-start = (f32[4,8,16,8,128]{4,3,2,1,0:T(8,128)S(1)}, f32[4,8,16,8,128]{4,3,2,1,0:T(8,128)}, u32[]{:S(2)}, u32[]{:S(2)}) collective-permute-start(f32[4,8,16,8,128]{4,3,2,1,0:T(8,128)S(1)} %other_b.1.rest_0_), channel_id=1, source_target_pairs={{0,64},{64,0},{1,65},{65,1},{2,66},{66,2},{3,67},{67,3},{4,68},{68... | collective-permute-start | bytes 6291464 | tf_op jit(solution)/shard_map/ppermute | solution.py:280
  11.3 7.0 %collective-permute-start.1 = (f32[8,128]{1,0:T(8,128)S(1)}, f32[8,128]{1,0:T(8,128)S(1)}, u32[]{:S(2)}, u32[]{:S(2)}) collective-permute-start(f32[8,128]{1,0:T(8,128)S(1)} %pad.4.here), channel_id=1, source_target_pairs={{0,8},{8,0},{1,9},{9,1},{2,10},{10,2},{3,11},{11,3},{4,12},{12,4},... | collective-permute-start | bytes 12296 | tf_op jit(solution)/shard_map/ppermute | solution.py:280
  15.9 0.8 copy-start.1
  16.8 0.8 copy-start.2
  17.6 0.8 copy-start.3
  23.5 30.8 %copy-start.8 = (s32[128]{0:T(128)S(1)}, s32[128]{0:T(128)}, u32[]{:S(2)}) copy-start(s32[128]{0:T(128)} %param.6) | copy-start | bytes 1540
  23.5 30.8 %all-to-all-start = ((f32[8,65,8,128]{3,2,1,0:T(8,128)}), f32[8,65,8,128]{3,2,1,0:T(8,128)S(1)}, u32[]{:S(2)}, u32[]{:S(2)}) async-start(f32[8,65,8,128]{3,2,1,0:T(8,128)} %mine_b.1), calls=%async_computation | async-start | bytes 4259840 | tf_op jit(solution)/shard_map/all_to_all | solution.py:307
  27.8 32.3 %collective-permute-start.3 = (f32[8,16,8,128]{3,2,1,0:T(8,128)}, f32[8,16,8,128]{3,2,1,0:T(8,128)S(1)}, u32[]{:S(2)}, u32[]{:S(2)}) collective-permute-start(f32[8,16,8,128]{3,2,1,0:T(8,128)} %copy-done.3), channel_id=1, source_target_pairs={{0,8},{8,0},{128,136},{136,128},{1,9},{9,1},{129,137},{137,129},{2... | collective-permute-start | bytes 1572872 | tf_op jit(solution)/shard_map/ppermute | solution.py:280
  28.5 31.6 %collective-permute-start.4 = (f32[8,16,8,128]{3,2,1,0:T(8,128)}, f32[8,16,8,128]{3,2,1,0:T(8,128)}, u32[]{:S(2)}, u32[]{:S(2)}) collective-permute-start(f32[8,16,8,128]{3,2,1,0:T(8,128)} %copy-done.2), channel_id=1, source_target_pairs={{0,128},{8,136},{128,0},{136,8},{1,129},{9,137},{129,1},{137,9},{2... | collective-permute-start | bytes 1572872 | tf_op jit(solution)/shard_map/ppermute | solution.py:280
  31.1 29.0 %collective-permute-start.5 = (f32[8,16,8,128]{3,2,1,0:T(8,128)}, f32[8,16,8,128]{3,2,1,0:T(8,128)}, u32[]{:S(2)}, u32[]{:S(2)}) collective-permute-start(f32[8,16,8,128]{3,2,1,0:T(8,128)} %copy-done.1), channel_id=1, source_target_pairs={{0,136},{8,128},{128,8},{136,0},{1,137},{9,129},{129,9},{137,1},{2... | collective-permute-start | bytes 1572872 | tf_op jit(solution)/shard_map/ppermute | solution.py:280
  58.0 0.7 copy-start.4
  58.8 0.7 copy-start.6
  59.4 0.7 copy-start.9
  60.1 7.4 %copy-start.7 = (f32[4,128,128]{2,1,0:T(8,128)S(1)}, f32[4,128,128]{2,1,0:T(8,128)}, u32[]{:S(2)}) copy-start(f32[4,128,128]{2,1,0:T(8,128)} %copy-done.6) | copy-start | bytes 786436
  60.2 8.4 %copy-start.5 = (f32[4,128,128]{2,1,0:T(8,128)S(1)}, f32[4,128,128]{2,1,0:T(8,128)}, u32[]{:S(2)}) copy-start(f32[4,128,128]{2,1,0:T(8,128)} %copy-done.4) | copy-start | bytes 786436
  60.2 24.2 %copy-start.10 = (f32[4,128,128]{2,1,0:T(8,128)S(1)}, f32[4,128,128]{2,1,0:T(8,128)}, u32[]{:S(2)}) copy-start(f32[4,128,128]{2,1,0:T(8,128)} %copy-done.9) | copy-start | bytes 786436
  63.7 20.7 %all-to-all-start.1 = ((f32[8,2,16,8,128]{4,3,2,1,0:T(8,128)}), f32[8,2,16,8,128]{4,3,2,1,0:T(8,128)S(1)}, u32[]{:S(2)}, u32[]{:S(2)}) async-start(f32[8,2,16,8,128]{4,3,2,1,0:T(8,128)} %sum_a.1), calls=%async_computation.1 | async-start | bytes 2097152 | tf_op jit(solution)/shard_map/all_to_all | solution.py:311
  67.6 6.3 %collective-permute-start.6 = (f32[4,128,128]{2,1,0:T(8,128)S(1)}, f32[4,128,128]{2,1,0:T(8,128)S(1)}, u32[]{:S(2)}, u32[]{:S(2)}) collective-permute-start(f32[4,128,128]{2,1,0:T(8,128)S(1)} %copy-done.7), channel_id=1, source_target_pairs={{0,8},{8,0},{128,136},{136,128},{1,9},{9,1},{129,137},{137,129},{2... | collective-permute-start | bytes 786440 | tf_op jit(solution)/shard_map/ppermute | solution.py:280
  68.6 12.9 %collective-permute-start.7 = (f32[4,128,128]{2,1,0:T(8,128)S(1)}, f32[4,128,128]{2,1,0:T(8,128)S(1)}, u32[]{:S(2)}, u32[]{:S(2)}) collective-permute-start(f32[4,128,128]{2,1,0:T(8,128)S(1)} %copy-done.5), channel_id=1, source_target_pairs={{0,128},{8,136},{128,0},{136,8},{1,129},{9,137},{129,1},{137,9},{2... | collective-permute-start | bytes 786440 | tf_op jit(solution)/shard_map/ppermute | solution.py:280
  71.0 13.4 %collective-permute-start.8 = (f32[4,128,128]{2,1,0:T(8,128)S(1)}, f32[4,128,128]{2,1,0:T(8,128)S(1)}, u32[]{:S(2)}, u32[]{:S(2)}) collective-permute-start(f32[4,128,128]{2,1,0:T(8,128)S(1)} %get-tuple-element.26), channel_id=1, source_target_pairs={{0,136},{8,128},{128,8},{136,0},{1,137},{9,129},{129,9},{137,1},{2... | collective-permute-start | bytes 786440 | tf_op jit(solution)/shard_map/ppermute | solution.py:280
  87.2 8.5 %collective-permute-start.10 = (f32[2,128,128]{2,1,0:T(8,128)S(1)}, f32[2,128,128]{2,1,0:T(8,128)S(1)}, u32[]{:S(2)}, u32[]{:S(2)}) collective-permute-start(f32[2,128,128]{2,1,0:T(8,128)S(1)} %get-tuple-element.29), channel_id=1, source_target_pairs={{0,4},{2,6},{4,0},{6,2},{1,5},{3,7},{5,1},{7,3},{8,12},{10,14},{12... | collective-permute-start | bytes 393224 | tf_op jit(solution)/shard_map/ppermute | solution.py:289
  93.3 13.6 %collective-permute-start.11 = (f32[2,128,128]{2,1,0:T(8,128)S(1)}, f32[2,128,128]{2,1,0:T(8,128)S(1)}, u32[]{:S(2)}, u32[]{:S(2)}) collective-permute-start(f32[2,128,128]{2,1,0:T(8,128)S(1)} %get-tuple-element.30), channel_id=1, source_target_pairs={{0,6},{2,0},{4,2},{6,4},{1,7},{3,1},{5,3},{7,5},{8,14},{10,8},{12,... | collective-permute-start | bytes 393224 | tf_op jit(solution)/shard_map/ppermute | solution.py:289
  93.6 13.3 %collective-permute-start.9 = (f32[2,128,128]{2,1,0:T(8,128)S(1)}, f32[2,128,128]{2,1,0:T(8,128)S(1)}, u32[]{:S(2)}, u32[]{:S(2)}) collective-permute-start(f32[2,128,128]{2,1,0:T(8,128)S(1)} %get-tuple-element.28), channel_id=1, source_target_pairs={{0,2},{2,4},{4,6},{6,0},{1,3},{3,5},{5,7},{7,1},{8,10},{10,12},{12... | collective-permute-start | bytes 393224 | tf_op jit(solution)/shard_map/ppermute | solution.py:289

commit v3 on v2

--- a/solution.py
+++ b/solution.py
@@ -114,7 +114,7 @@
         ),
         out_shape=out_shape,
         name=("other" if other is None else "mine") + ("_a", "_b")[chunk],
-        **params(2 * 256 * 2048 * 1024, 7 << 20, 50),
+        **params(2 * 256 * 2048 * 1024, 7 << 20, 46),
     )(index, tables, traces, *([] if other is None else [other]), *places, *after)
 
 
@@ -125,12 +125,10 @@
 
 
 def sum_a(parts, after=()):
-    spec = pl.BlockSpec((2, PAIRS, 8, 128), lambda i: (i, 0, 0, 0))
     return pl.pallas_call(
         sum_a_body,
-        grid=(N_XZ // 2,),
-        in_specs=[spec] * N_Y + [ANY] * len(after),
-        out_specs=pl.BlockSpec((2, 2, PAIRS, 8, 128), lambda i: (i, 0, 0, 0, 0)),
+        in_specs=[WHOLE] * N_Y + [ANY] * len(after),
+        out_specs=WHOLE,
         out_shape=jax.ShapeDtypeStruct((N_XZ, 2, PAIRS, 8, 128), jnp.float32),
         name="sum_a",
         **params(1 << 18, 3 << 20),
@@ -199,8 +197,8 @@
     return res[:NP] + jnp.where(left, cross, -cross)
 
 
-def slant_a_body(zh, base, yh, yl, slowness, places, data, *rest):
-    parts, outs, (slow, high, low) = rest[:N_Y], rest[N_Y : N_Y + N_ZH], rest[N_Y + N_ZH :]
+def slant_a_body(n_after, zh, base, yh, yl, slowness, places, data, *rest):
+    outs, (slow, high, low) = rest[n_after : n_after + N_ZH], rest[n_after + N_ZH :]
     for parity in range(2):
         for place in range(2):
             row = 2 * place + parity
@@ -212,20 +210,19 @@
         for part in range(2):
             rows = [data[:, pl.ds(place * PAIRS * 8 + 2 * j + part, PAIRS, stride=8), :] for place in range(2)]
             cols.append(jnp.concatenate([row.reshape(N_XZ * PAIRS, 128) for row in rows], axis=0))
-        out[0] = stack(high[j], low[j], *cols)
-        out[1] = (parts[0][j] + parts[1][j]) + (parts[2][j] + parts[3][j])
-
-
-def slant_a(zh, base, yh, yl, slowness, places, data, parts):
-    return pl.pallas_call(
-        slant_a_body,
-        in_specs=[SCALAR] * 4 + [WHOLE] * (3 + N_Y),
+        out[...] = stack(high[j], low[j], *cols)
+
+
+def slant_a(zh, base, yh, yl, slowness, places, data, after=()):
+    return pl.pallas_call(
+        functools.partial(slant_a_body, len(after)),
+        in_specs=[SCALAR] * 4 + [WHOLE] * 3 + [ANY] * len(after),
         out_specs=[WHOLE] * N_ZH,
-        out_shape=[jax.ShapeDtypeStruct((2, NP, 128), jnp.float32)] * N_ZH,
+        out_shape=[jax.ShapeDtypeStruct((NP, 128), jnp.float32)] * N_ZH,
         scratch_shapes=[pltpu.VMEM((NP, 128), jnp.int32)] + [pltpu.VMEM((N_ZH, 2 * NP, 512), jnp.bfloat16)] * 2,
         name="slant_a",
         **params(1 << 30, 5 << 20),
-    )(zh, base, yh, yl, slowness, places, data.reshape(N_XZ, 2 * PAIRS * 8, 128), *parts)
+    )(zh, base, yh, yl, slowness, places, data.reshape(N_XZ, 2 * PAIRS * 8, 128), *after)
 
 
 def slant_b_body(n_after, base, yh, yl, slowness, data, *rest):
@@ -256,11 +253,29 @@
     )(base, yh, yl, slowness, data.reshape(N_XZ, (N_Y * PAIRS + 1) * 8, 128), *after)
 
 
-def finish_body(own, *rest):
+def sum_b_body(zh, own, yl, yh, both, *rest):
+    outs = rest[-N_ZH:]
+    for e, out in enumerate(outs):
+        j = (zh[0] + e) & (N_ZH - 1)
+        out[...] = (own[j] + yl[j]) + (yh[j] + both[j])
+
+
+def sum_b(zh, parts, after=()):
+    return pl.pallas_call(
+        sum_b_body,
+        in_specs=[SCALAR] + [WHOLE] * N_Y + [ANY] * len(after),
+        out_specs=[WHOLE] * N_ZH,
+        out_shape=[jax.ShapeDtypeStruct((NP, 128), jnp.float32)] * N_ZH,
+        name="sum_b",
+        **params(1 << 18, 1 << 20),
+    )(zh, *parts, *after)
+
+
+def finish_body(*refs):
     scale = jnp.float32(1.0 / math.sqrt(NT) / math.sqrt(SHOTS))
     left = lax.broadcasted_iota(jnp.int32, (NP, 128), 1) < HALF
-    out = rest[-1]
-    a, b = (((own[i] + rest[0][i]) + (rest[1][i] + rest[2][i])) * scale for i in range(2))
+    total = lambda four: ((four[0][...] + four[1][...]) + (four[2][...] + four[3][...])) * scale
+    a, b, out = total(refs[:4]), total(refs[4:8]), refs[8]
     out[0, 0] = jnp.where(left, a, pltpu.roll(b, HALF, 1))
     out[0, 1] = jnp.where(left, pltpu.roll(a, HALF, 1), b)
 
@@ -268,7 +283,7 @@
 def finish(parts):
     return pl.pallas_call(
         finish_body,
-        in_specs=[WHOLE] * N_ZH,
+        in_specs=[WHOLE] * 8,
         out_specs=WHOLE,
         out_shape=jax.ShapeDtypeStruct((1, 2, NP, REC), jnp.float32),
         name="finish",
@@ -305,11 +320,15 @@
     there = swap(places, "yl", 2, 1)
     mine_b = dft(index, tables, traces, 0, 1, swap(other_b, "c", 2, 1), after=[mine_a[0]], places=[places, there])
     data_b = lax.all_to_all(mine_b, ("x", "zl"), 0, 0, tiled=True)
+    both_a = sum_a(exchange_y(mine_a), after=[mine_b])
+    data_a = lax.all_to_all(both_a, ("x", "zl"), 0, 0, tiled=True)
 
     where = one(FREQ0 + c * 64 + x * 16 + zl), one(yh), one(yl), slowness.reshape(1, NP)
-    *part_b, places = slant_b(*where, data_b)
-    data_a = lax.all_to_all(sum_a(exchange_y(mine_a), after=[places]), ("x", "zl"), 0, 0, tiled=True)
-    return finish(exchange_z(slant_a(one(zh), *where, places, data_a, exchange_y(part_b))))
+    *part_b, places = slant_b(*where, data_b, after=[both_a])
+    part_b = exchange_y(part_b)
+    part_a = slant_a(one(zh), *where, places, data_a)
+    part_b = sum_b(one(zh), part_b, after=[part_a[0]])
+    return finish([*exchange_z(part_a), *exchange_z(part_b)])
 
 
 def solution(mesh):

time: 108 us -> 98.7 us (0.914)
  the two profiles are of different devices: /device:TPU:1 before, /device:TPU:64 now
where the time goes in v3:
time: 98.7 us; the launch traced here: 98.6 us
  waiting for transfers between devices  35.4 us (36%)
  starting transfers between devices  35.3 us (36%)
  Pallas kernels  25.7 us (26%)
  local copies, waits for them, and re-layouts  2.05 us (2%)
    ppermute x9, waiting for transfers between devices, swap(): return lax.ppermute(value, axes, [(i, i ^ mask) for i in range(size)])  24.1 us
    pallas_call x4, Pallas kernels, dft(): pl.pallas_call(functools.partial(body, len(after)), grid_spec=pltpu.Prefe...  16.4 us
    ppermute x6, starting transfers between devices, exchange_z(): lax.ppermute(parts[e], 'zh', shift(e))  13.8 us
    ppermute x9, starting transfers between devices, swap(): return lax.ppermute(value, axes, [(i, i ^ mask) for i in range(size)])  10.4 us
    ppermute x6, waiting for transfers between devices, exchange_z(): lax.ppermute(parts[e], 'zh', shift(e))  7.06 us
    all_to_all x1, starting transfers between devices, body(): data_b = lax.all_to_all(mine_b, ('x', 'zl'), 0, 0, tiled=True)  5.66 us
    all_to_all x1, starting transfers between devices, body(): data_a = lax.all_to_all(both_a, ('x', 'zl'), 0, 0, tiled=True)  5.42 us
    pallas_call x1, Pallas kernels, slant_b(): pl.pallas_call(functools.partial(slant_b_body, len(after)), in_specs=[SCA...  4.61 us
  transfers between devices with their start and end apart: 17, of which 6 were waited for; matrix products, arithmetic and copies ran while one was open for 0% of the time, Pallas kernels for 16%

profile of v3, /device:TPU:64, one launch (start us, length us, event | category | flops | bytes accessed | tf_op | source)
XLA Modules:
  0.0 98.6 jit_solution(292996214980576081)
XLA Ops:
  0.0 4.2 %other_a.1.rest_0_ = f32[4,8,16,8,128]{4,3,2,1,0:T(8,128)} custom-call(s32[1]{0:T(128)} %bitcast.5.index, bf16[8,2,256,1024]{3,2,1,0:T(8,128)(2,1)} %constant.36.clone.table, bf16[32,128,1024]{2,1,0:T(8,128)(2,1)} %traces.7), custom_call_target="tpu_custom_call" | custom-call | flops 1073741824 | bytes 7340032 | tf_op jit(solution)/shard_map/other_a/pallas_call | solution.py:101
  4.2 0.0 copy-start.3
  4.2 0.0 collective-permute-start.2
  4.2 3.3 %other_b.1.rest_0_ = f32[4,8,16,8,128]{4,3,2,1,0:T(8,128)S(1)} custom-call(s32[1]{0:T(128)} %bitcast.5.index, bf16[8,2,256,1024]{3,2,1,0:T(8,128)(2,1)} %constant.36.clone.table, bf16[32,128,1024]{2,1,0:T(8,128)(2,1)} %traces.7, f32[4,8,16,8,128]{4,3,2,1,0:T(8,128)} %other_a.1.rest_0_), custom_call_target="tpu_custom_call" | custom-call | flops 1073741824 | bytes 7340032 | tf_op jit(solution)/shard_map/other_b/pallas_call | solution.py:101
  7.6 0.6 collective-permute-start
  8.2 0.1 mul.45
  8.2 0.1 mul.46
  8.3 0.0 copy-done.3
  8.3 0.1 mul.41
  8.4 0.1 copy.6
  8.5 0.1 mul.43
  8.6 1.7 %collective-permute-start.1 = (f32[8,128]{1,0:T(8,128)S(1)}, f32[8,128]{1,0:T(8,128)S(1)}, u32[]{:S(2)}, u32[]{:S(2)}) collective-permute-start(f32[8,128]{1,0:T(8,128)S(1)} %pad.4.here), channel_id=1, source_target_pairs={{0,8},{8,0},{1,9},{9,1},{2,10},{10,2},{3,11},{11,3},{4,12},{12,4},... | collective-permute-start | bytes 12296 | tf_op jit(solution)/shard_map/ppermute | solution.py:295
  10.3 0.0 collective-permute-done.2.other
  10.3 3.8 %mine_a.1 = (f32[8,16,8,128]{3,2,1,0:T(8,128)S(1)}, f32[8,16,8,128]{3,2,1,0:T(8,128)S(1)}, f32[8,16,8,128]{3,2,1,0:T(8,128)S(1)}, f32[8,16,8,128]{3,2,1,0:T(8,128)S(1)}) custom-call(s32[1]{0:T(128)} %bitcast.5.index, bf16[8,2,256,1024]{3,2,1,0:T(8,128)(2,1)} %constant.36.clone.table, bf16[32,128,1024]{2,1,0:T(8,128)(2,1)} %traces.7, ...), custom_call_target="tpu_custom_call" | custom-call | flops 1073741824 | bytes 7340032 | tf_op jit(solution)/shard_map/mine_a/pallas_call | solution.py:101
  14.1 0.0 copy-start
  14.1 0.8 copy-done
  14.9 0.0 copy-start.1
  14.9 0.8 copy-done.1
  15.7 0.0 collective-permute-done.1.there
  15.7 0.0 collective-permute-done.other
  15.7 5.0 %mine_b.1.rest_0_ = f32[8,65,8,128]{3,2,1,0:T(8,128)} custom-call(s32[1]{0:T(128)} %bitcast.5.index, bf16[8,2,256,1024]{3,2,1,0:T(8,128)(2,1)} %constant.36.clone.table, bf16[32,128,1024]{2,1,0:T(8,128)(2,1)} %traces.7, f32[4,8,16,8,128]{4,3,2,1,0:T(8,128)} %collective-permute-done.other, f32[8,128]{1,0:T(8,128)S(1)} %pad.4.here, ...), custom_call_target="tpu_custom_call" | custom-call | flops 1073741824 | bytes 7340032 | tf_op jit(solution)/shard_map/mine_b/pallas_call | solution.py:101
  20.7 5.7 %all-to-all-start = ((f32[8,65,8,128]{3,2,1,0:T(8,128)}), f32[8,65,8,128]{3,2,1,0:T(8,128)S(1)}, u32[]{:S(2)}, u32[]{:S(2)}) async-start(f32[8,65,8,128]{3,2,1,0:T(8,128)} %mine_b.1.rest_0_), calls=%async_computation | async-start | bytes 4259840 | tf_op jit(solution)/shard_map/all_to_all | solution.py:322
  26.4 0.4 collective-permute-start.3
  26.8 3.2 %collective-permute-start.4 = (f32[8,16,8,128]{3,2,1,0:T(8,128)}, f32[8,16,8,128]{3,2,1,0:T(8,128)S(1)}, u32[]{:S(2)}, u32[]{:S(2)}) collective-permute-start(f32[8,16,8,128]{3,2,1,0:T(8,128)} %copy-done), channel_id=1, source_target_pairs={{0,128},{8,136},{128,0},{136,8},{1,129},{9,137},{129,1},{137,9},{2... | collective-permute-start | bytes 1572872 | tf_op jit(solution)/shard_map/ppermute | solution.py:295
  30.0 0.0 copy-start.2
  30.0 1.1 %collective-permute-start.5 = (f32[8,16,8,128]{3,2,1,0:T(8,128)S(1)}, f32[8,16,8,128]{3,2,1,0:T(8,128)S(1)}, u32[]{:S(2)}, u32[]{:S(2)}) collective-permute-start(f32[8,16,8,128]{3,2,1,0:T(8,128)S(1)} %get-tuple-element.25), channel_id=1, source_target_pairs={{0,136},{8,128},{128,8},{136,0},{1,137},{9,129},{129,9},{137,1},{2... | collective-permute-start | bytes 1572872 | tf_op jit(solution)/shard_map/ppermute | solution.py:295
  31.1 10.4 %collective-permute-done.3.yl = f32[8,16,8,128]{3,2,1,0:T(8,128)S(1)} collective-permute-done((f32[8,16,8,128]{3,2,1,0:T(8,128)}, f32[8,16,8,128]{3,2,1,0:T(8,128)S(1)}, u32[]{:S(2)}, u32[]{:S(2)}) %collective-permute-start.3) | collective-permute-done | bytes 524320 | tf_op jit(solution)/shard_map/ppermute | solution.py:295
  41.4 11.4 %collective-permute-done.4.yh = f32[8,16,8,128]{3,2,1,0:T(8,128)S(1)} collective-permute-done((f32[8,16,8,128]{3,2,1,0:T(8,128)}, f32[8,16,8,128]{3,2,1,0:T(8,128)S(1)}, u32[]{:S(2)}, u32[]{:S(2)}) %collective-permute-start.4) | collective-permute-done | bytes 524320 | tf_op jit(solution)/shard_map/ppermute | solution.py:295
  52.8 2.4 %collective-permute-done.5.both = f32[8,16,8,128]{3,2,1,0:T(8,128)S(1)} collective-permute-done((f32[8,16,8,128]{3,2,1,0:T(8,128)S(1)}, f32[8,16,8,128]{3,2,1,0:T(8,128)S(1)}, u32[]{:S(2)}, u32[]{:S(2)}) %collective-permute-start.5) | collective-permute-done | bytes 524320 | tf_op jit(solution)/shard_map/ppermute | solution.py:295
  55.2 1.1 %sum_a.1.rest_0_ = f32[8,2,16,8,128]{4,3,2,1,0:T(8,128)} custom-call(f32[8,16,8,128]{3,2,1,0:T(8,128)S(1)} %get-tuple-element.22.rest_0_.own, f32[8,16,8,128]{3,2,1,0:T(8,128)S(1)} %collective-permute-done.3.yl, f32[8,16,8,128]{3,2,1,0:T(8,128)S(1)} %collective-permute-done.4.yh, f32[8,16,8,128]{3,2,1,0:T(8,128)S(1)} %collective-permute-done.5.both, ...), custom_call_target="tpu_custom_call" | custom-call | flops 262144 | bytes 3145728 | tf_op jit(solution)/shard_map/sum_a/pallas_call | solution.py:128
  56.3 0.0 all-to-all-done
  56.3 5.4 %all-to-all-start.1 = ((f32[8,2,16,8,128]{4,3,2,1,0:T(8,128)}), f32[8,2,16,8,128]{4,3,2,1,0:T(8,128)S(1)}, u32[]{:S(2)}, u32[]{:S(2)}) async-start(f32[8,2,16,8,128]{4,3,2,1,0:T(8,128)} %sum_a.1.rest_0_), calls=%async_computation.1 | async-start | bytes 2097152 | tf_op jit(solution)/shard_map/all_to_all | solution.py:324
  61.7 0.0 copy-done.2
  61.7 4.6 %slant_b.1 = (f32[4,128,128]{2,1,0:T(8,128)S(1)}, f32[4,128,128]{2,1,0:T(8,128)}, f32[4,128,128]{2,1,0:T(8,128)}, f32[4,128,128]{2,1,0:T(8,128)}, f32[8,128]{1,0:T(8,128)S(1)}) custom-call(s32[1]{0:T(128)} %bitcast.1.base, s32[1]{0:T(128)} %bitcast.2.yh, s32[1]{0:T(128)} %bitcast.3.yl, s32[1,128]{1,0:T(1,128)S(1)} %bitcast.14, f32[8,520,128]{2,1,0:T(8,128)S(1)} %bitcast.12, ...), custom_call_target="tpu_custom_call" | custom-call | flops 2147483648 | bytes 7340032 | tf_op jit(solution)/shard_map/slant_b/pallas_call | solution.py:245
  66.4 0.0 collective-permute-start.10
  66.4 2.1 %collective-permute-start.11 = (f32[4,128,128]{2,1,0:T(8,128)}, f32[4,128,128]{2,1,0:T(8,128)S(1)}, u32[]{:S(2)}, u32[]{:S(2)}) collective-permute-start(f32[4,128,128]{2,1,0:T(8,128)} %get-tuple-element.34), channel_id=1, source_target_pairs={{0,136},{8,128},{128,8},{136,0},{1,137},{9,129},{129,9},{137,1},{2... | collective-permute-start | bytes 786440 | tf_op jit(solution)/shard_map/ppermute | solution.py:295
  68.5 1.3 %collective-permute-start.9 = (f32[4,128,128]{2,1,0:T(8,128)}, f32[4,128,128]{2,1,0:T(8,128)S(1)}, u32[]{:S(2)}, u32[]{:S(2)}) collective-permute-start(f32[4,128,128]{2,1,0:T(8,128)} %get-tuple-element.32), channel_id=1, source_target_pairs={{0,8},{8,0},{128,136},{136,128},{1,9},{9,1},{129,137},{137,129},{2... | collective-permute-start | bytes 786440 | tf_op jit(solution)/shard_map/ppermute | solution.py:295
  69.8 4.2 %all-to-all-done.1 = f32[8,2,16,8,128]{4,3,2,1,0:T(8,128)S(1)} async-done(((f32[8,2,16,8,128]{4,3,2,1,0:T(8,128)}), f32[8,2,16,8,128]{4,3,2,1,0:T(8,128)S(1)}, u32[]{:S(2)}, u32[]{:S(2)}) %all-to-all-start.1) | async-done | bytes 1048608 | tf_op jit(solution)/shard_map/all_to_all | solution.py:324
  74.0 2.8 %slant_a.1 = (f32[128,128]{1,0:T(8,128)S(1)}, f32[128,128]{1,0:T(8,128)S(1)}, f32[128,128]{1,0:T(8,128)S(1)}, f32[128,128]{1,0:T(8,128)S(1)}) custom-call(s32[1]{0:T(128)} %bitcast.zh, s32[1]{0:T(128)} %bitcast.1.base, s32[1]{0:T(128)} %bitcast.2.yh, s32[1]{0:T(128)} %bitcast.3.yl, s32[1,128]{1,0:T(1,128)S(1)} %bitcast.15, ...), custom_call_target="tpu_custom_call" | custom-call | flops 1073741824 | bytes 5242880 | tf_op jit(solution)/shard_map/slant_a/pallas_call | solution.py:217
  76.8 3.6 %collective-permute-start.6 = (f32[128,128]{1,0:T(8,128)S(1)}, f32[128,128]{1,0:T(8,128)S(1)}, u32[]{:S(2)}, u32[]{:S(2)}) collective-permute-start(f32[128,128]{1,0:T(8,128)S(1)} %get-tuple-element.28), channel_id=1, source_target_pairs={{0,2},{2,4},{4,6},{6,0},{1,3},{3,5},{5,7},{7,1},{8,10},{10,12},{12... | collective-permute-start | bytes 196616 | tf_op jit(solution)/shard_map/ppermute | solution.py:304
  80.5 1.2 %collective-permute-start.7 = (f32[128,128]{1,0:T(8,128)S(1)}, f32[128,128]{1,0:T(8,128)S(1)}, u32[]{:S(2)}, u32[]{:S(2)}) collective-permute-start(f32[128,128]{1,0:T(8,128)S(1)} %get-tuple-element.29), channel_id=1, source_target_pairs={{0,4},{2,6},{4,0},{6,2},{1,5},{3,7},{5,1},{7,3},{8,12},{10,14},{12... | collective-permute-start | bytes 196616 | tf_op jit(solution)/shard_map/ppermute | solution.py:304
  81.7 0.0 collective-permute-done.10.yh
  81.7 2.6 %collective-permute-start.8 = (f32[128,128]{1,0:T(8,128)S(1)}, f32[128,128]{1,0:T(8,128)S(1)}, u32[]{:S(2)}, u32[]{:S(2)}) collective-permute-start(f32[128,128]{1,0:T(8,128)S(1)} %get-tuple-element.30), channel_id=1, source_target_pairs={{0,6},{2,0},{4,2},{6,4},{1,7},{3,1},{5,3},{7,5},{8,14},{10,8},{12,... | collective-permute-start | bytes 196616 | tf_op jit(solution)/shard_map/ppermute | solution.py:304
  84.3 0.0 collective-permute-done.11.both
  84.3 0.0 collective-permute-done.9.yl
  84.3 0.1 sum_b.1
  84.4 1.6 %collective-permute-start.12 = (f32[128,128]{1,0:T(8,128)S(1)}, f32[128,128]{1,0:T(8,128)S(1)}, u32[]{:S(2)}, u32[]{:S(2)}) collective-permute-start(f32[128,128]{1,0:T(8,128)S(1)} %get-tuple-element.36), channel_id=1, source_target_pairs={{0,2},{2,4},{4,6},{6,0},{1,3},{3,5},{5,7},{7,1},{8,10},{10,12},{12... | collective-permute-start | bytes 196616 | tf_op jit(solution)/shard_map/ppermute | solution.py:304
  86.0 4.7 %collective-permute-start.13 = (f32[128,128]{1,0:T(8,128)S(1)}, f32[128,128]{1,0:T(8,128)S(1)}, u32[]{:S(2)}, u32[]{:S(2)}) collective-permute-start(f32[128,128]{1,0:T(8,128)S(1)} %get-tuple-element.37), channel_id=1, source_target_pairs={{0,4},{2,6},{4,0},{6,2},{1,5},{3,7},{5,1},{7,3},{8,12},{10,14},{12... | collective-permute-start | bytes 196616 | tf_op jit(solution)/shard_map/ppermute | solution.py:304
  90.7 0.0 collective-permute-done.6.refs_1_
  90.7 0.0 collective-permute-start.14
  90.7 0.0 collective-permute-done.7.refs_2_
  90.7 0.0 collective-permute-done.8.refs_3_
  90.7 0.0 collective-permute-done.12.refs_5_
  90.7 3.4 %collective-permute-done.13.refs_6_ = f32[128,128]{1,0:T(8,128)S(1)} collective-permute-done((f32[128,128]{1,0:T(8,128)S(1)}, f32[128,128]{1,0:T(8,128)S(1)}, u32[]{:S(2)}, u32[]{:S(2)}) %collective-permute-start.13) | collective-permute-done | bytes 65568 | tf_op jit(solution)/shard_map/ppermute | solution.py:304
  94.1 3.6 %collective-permute-done.14.refs_7_ = f32[128,128]{1,0:T(8,128)S(1)} collective-permute-done((f32[128,128]{1,0:T(8,128)S(1)}, f32[128,128]{1,0:T(8,128)S(1)}, u32[]{:S(2)}, u32[]{:S(2)}) %collective-permute-start.14) | collective-permute-done | bytes 65568 | tf_op jit(solution)/shard_map/ppermute | solution.py:304
  97.8 0.8 finish.1
  (4 shorter events, 0.0 us)
Async XLA Ops:
  4.2 4.1 %copy-start.3 = (s32[32]{0:T(128)S(1)}, s32[32]{0:T(128)}, u32[]{:S(2)}) copy-start(s32[32]{0:T(128)} %param.5) | copy-start | bytes 388
  4.2 6.0 %collective-permute-start.2 = (f32[4,8,16,8,128]{4,3,2,1,0:T(8,128)}, f32[4,8,16,8,128]{4,3,2,1,0:T(8,128)}, u32[]{:S(2)}, u32[]{:S(2)}) collective-permute-start(f32[4,8,16,8,128]{4,3,2,1,0:T(8,128)} %other_a.1.rest_0_), channel_id=1, source_target_pairs={{0,64},{64,0},{1,65},{65,1},{2,66},{66,2},{3,67},{67,3},{4,68},{68... | collective-permute-start | bytes 6291464 | tf_op jit(solution)/shard_map/ppermute | solution.py:295
  7.6 8.1 %collective-permute-start = (f32[4,8,16,8,128]{4,3,2,1,0:T(8,128)S(1)}, f32[4,8,16,8,128]{4,3,2,1,0:T(8,128)}, u32[]{:S(2)}, u32[]{:S(2)}) collective-permute-start(f32[4,8,16,8,128]{4,3,2,1,0:T(8,128)S(1)} %other_b.1.rest_0_), channel_id=1, source_target_pairs={{0,64},{64,0},{1,65},{65,1},{2,66},{66,2},{3,67},{67,3},{4,68},{68... | collective-permute-start | bytes 6291464 | tf_op jit(solution)/shard_map/ppermute | solution.py:295
  8.6 7.1 %collective-permute-start.1 = (f32[8,128]{1,0:T(8,128)S(1)}, f32[8,128]{1,0:T(8,128)S(1)}, u32[]{:S(2)}, u32[]{:S(2)}) collective-permute-start(f32[8,128]{1,0:T(8,128)S(1)} %pad.4.here), channel_id=1, source_target_pairs={{0,8},{8,0},{1,9},{9,1},{2,10},{10,2},{3,11},{11,3},{4,12},{12,4},... | collective-permute-start | bytes 12296 | tf_op jit(solution)/shard_map/ppermute | solution.py:295
  14.1 0.8 copy-start
  14.9 0.8 copy-start.1
  20.7 35.6 %all-to-all-start = ((f32[8,65,8,128]{3,2,1,0:T(8,128)}), f32[8,65,8,128]{3,2,1,0:T(8,128)S(1)}, u32[]{:S(2)}, u32[]{:S(2)}) async-start(f32[8,65,8,128]{3,2,1,0:T(8,128)} %mine_b.1.rest_0_), calls=%async_computation | async-start | bytes 4259840 | tf_op jit(solution)/shard_map/all_to_all | solution.py:322
  26.4 15.1 %collective-permute-start.3 = (f32[8,16,8,128]{3,2,1,0:T(8,128)}, f32[8,16,8,128]{3,2,1,0:T(8,128)S(1)}, u32[]{:S(2)}, u32[]{:S(2)}) collective-permute-start(f32[8,16,8,128]{3,2,1,0:T(8,128)} %copy-done.1), channel_id=1, source_target_pairs={{0,8},{8,0},{128,136},{136,128},{1,9},{9,1},{129,137},{137,129},{2... | collective-permute-start | bytes 1572872 | tf_op jit(solution)/shard_map/ppermute | solution.py:295
  26.8 26.0 %collective-permute-start.4 = (f32[8,16,8,128]{3,2,1,0:T(8,128)}, f32[8,16,8,128]{3,2,1,0:T(8,128)S(1)}, u32[]{:S(2)}, u32[]{:S(2)}) collective-permute-start(f32[8,16,8,128]{3,2,1,0:T(8,128)} %copy-done), channel_id=1, source_target_pairs={{0,128},{8,136},{128,0},{136,8},{1,129},{9,137},{129,1},{137,9},{2... | collective-permute-start | bytes 1572872 | tf_op jit(solution)/shard_map/ppermute | solution.py:295
  30.0 31.7 %copy-start.2 = (s32[128]{0:T(128)S(1)}, s32[128]{0:T(128)}, u32[]{:S(2)}) copy-start(s32[128]{0:T(128)} %param.6) | copy-start | bytes 1540
  30.0 25.2 %collective-permute-start.5 = (f32[8,16,8,128]{3,2,1,0:T(8,128)S(1)}, f32[8,16,8,128]{3,2,1,0:T(8,128)S(1)}, u32[]{:S(2)}, u32[]{:S(2)}) collective-permute-start(f32[8,16,8,128]{3,2,1,0:T(8,128)S(1)} %get-tuple-element.25), channel_id=1, source_target_pairs={{0,136},{8,128},{128,8},{136,0},{1,137},{9,129},{129,9},{137,1},{2... | collective-permute-start | bytes 1572872 | tf_op jit(solution)/shard_map/ppermute | solution.py:295
  56.3 17.7 %all-to-all-start.1 = ((f32[8,2,16,8,128]{4,3,2,1,0:T(8,128)}), f32[8,2,16,8,128]{4,3,2,1,0:T(8,128)S(1)}, u32[]{:S(2)}, u32[]{:S(2)}) async-start(f32[8,2,16,8,128]{4,3,2,1,0:T(8,128)} %sum_a.1.rest_0_), calls=%async_computation.1 | async-start | bytes 2097152 | tf_op jit(solution)/shard_map/all_to_all | solution.py:324
  66.4 15.3 %collective-permute-start.10 = (f32[4,128,128]{2,1,0:T(8,128)}, f32[4,128,128]{2,1,0:T(8,128)S(1)}, u32[]{:S(2)}, u32[]{:S(2)}) collective-permute-start(f32[4,128,128]{2,1,0:T(8,128)} %get-tuple-element.33), channel_id=1, source_target_pairs={{0,128},{8,136},{128,0},{136,8},{1,129},{9,137},{129,1},{137,9},{2... | collective-permute-start | bytes 786440 | tf_op jit(solution)/shard_map/ppermute | solution.py:295
  66.4 18.0 %collective-permute-start.11 = (f32[4,128,128]{2,1,0:T(8,128)}, f32[4,128,128]{2,1,0:T(8,128)S(1)}, u32[]{:S(2)}, u32[]{:S(2)}) collective-permute-start(f32[4,128,128]{2,1,0:T(8,128)} %get-tuple-element.34), channel_id=1, source_target_pairs={{0,136},{8,128},{128,8},{136,0},{1,137},{9,129},{129,9},{137,1},{2... | collective-permute-start | bytes 786440 | tf_op jit(solution)/shard_map/ppermute | solution.py:295
  68.5 15.8 %collective-permute-start.9 = (f32[4,128,128]{2,1,0:T(8,128)}, f32[4,128,128]{2,1,0:T(8,128)S(1)}, u32[]{:S(2)}, u32[]{:S(2)}) collective-permute-start(f32[4,128,128]{2,1,0:T(8,128)} %get-tuple-element.32), channel_id=1, source_target_pairs={{0,8},{8,0},{128,136},{136,128},{1,9},{9,1},{129,137},{137,129},{2... | collective-permute-start | bytes 786440 | tf_op jit(solution)/shard_map/ppermute | solution.py:295
  76.8 13.9 %collective-permute-start.6 = (f32[128,128]{1,0:T(8,128)S(1)}, f32[128,128]{1,0:T(8,128)S(1)}, u32[]{:S(2)}, u32[]{:S(2)}) collective-permute-start(f32[128,128]{1,0:T(8,128)S(1)} %get-tuple-element.28), channel_id=1, source_target_pairs={{0,2},{2,4},{4,6},{6,0},{1,3},{3,5},{5,7},{7,1},{8,10},{10,12},{12... | collective-permute-start | bytes 196616 | tf_op jit(solution)/shard_map/ppermute | solution.py:304
  80.5 10.2 %collective-permute-start.7 = (f32[128,128]{1,0:T(8,128)S(1)}, f32[128,128]{1,0:T(8,128)S(1)}, u32[]{:S(2)}, u32[]{:S(2)}) collective-permute-start(f32[128,128]{1,0:T(8,128)S(1)} %get-tuple-element.29), channel_id=1, source_target_pairs={{0,4},{2,6},{4,0},{6,2},{1,5},{3,7},{5,1},{7,3},{8,12},{10,14},{12... | collective-permute-start | bytes 196616 | tf_op jit(solution)/shard_map/ppermute | solution.py:304
  81.7 9.0 %collective-permute-start.8 = (f32[128,128]{1,0:T(8,128)S(1)}, f32[128,128]{1,0:T(8,128)S(1)}, u32[]{:S(2)}, u32[]{:S(2)}) collective-permute-start(f32[128,128]{1,0:T(8,128)S(1)} %get-tuple-element.30), channel_id=1, source_target_pairs={{0,6},{2,0},{4,2},{6,4},{1,7},{3,1},{5,3},{7,5},{8,14},{10,8},{12,... | collective-permute-start | bytes 196616 | tf_op jit(solution)/shard_map/ppermute | solution.py:304
  84.4 6.3 %collective-permute-start.12 = (f32[128,128]{1,0:T(8,128)S(1)}, f32[128,128]{1,0:T(8,128)S(1)}, u32[]{:S(2)}, u32[]{:S(2)}) collective-permute-start(f32[128,128]{1,0:T(8,128)S(1)} %get-tuple-element.36), channel_id=1, source_target_pairs={{0,2},{2,4},{4,6},{6,0},{1,3},{3,5},{5,7},{7,1},{8,10},{10,12},{12... | collective-permute-start | bytes 196616 | tf_op jit(solution)/shard_map/ppermute | solution.py:304
  86.0 8.2 %collective-permute-start.13 = (f32[128,128]{1,0:T(8,128)S(1)}, f32[128,128]{1,0:T(8,128)S(1)}, u32[]{:S(2)}, u32[]{:S(2)}) collective-permute-start(f32[128,128]{1,0:T(8,128)S(1)} %get-tuple-element.37), channel_id=1, source_target_pairs={{0,4},{2,6},{4,0},{6,2},{1,5},{3,7},{5,1},{7,3},{8,12},{10,14},{12... | collective-permute-start | bytes 196616 | tf_op jit(solution)/shard_map/ppermute | solution.py:304
  90.7 7.1 %collective-permute-start.14 = (f32[128,128]{1,0:T(8,128)S(1)}, f32[128,128]{1,0:T(8,128)S(1)}, u32[]{:S(2)}, u32[]{:S(2)}) collective-permute-start(f32[128,128]{1,0:T(8,128)S(1)} %get-tuple-element.38), channel_id=1, source_target_pairs={{0,6},{2,0},{4,2},{6,4},{1,7},{3,1},{5,3},{7,5},{8,14},{10,8},{12,... | collective-permute-start | bytes 196616 | tf_op jit(solution)/shard_map/ppermute | solution.py:304

commit v4 on v3

--- a/solution.py
+++ b/solution.py
@@ -114,7 +114,7 @@
         ),
         out_shape=out_shape,
         name=("other" if other is None else "mine") + ("_a", "_b")[chunk],
-        **params(2 * 256 * 2048 * 1024, 7 << 20, 46),
+        **params(2 * 256 * 2048 * 1024, 7 << 20, 44),
     )(index, tables, traces, *([] if other is None else [other]), *places, *after)
 
 
@@ -160,19 +160,20 @@
 def phase_tables(n_d, base, yh, yl, slowness, positions, column, slow, high, low):
     slow[...] = jnp.broadcast_to(slowness[...].astype(jnp.float32), (NP, 128)).T.astype(jnp.int32)
     first = base[0] + yh[0] * 128 + yl[0] * 8
-    rows = 16
+    rows = 32
 
     def step(i, _):
         row = pl.multiple_of(i * rows, rows)
         delay = (slow[pl.ds(row, rows), :] * positions) & (NT - 1)
-        own = turn(first * delay)
+        own, by_zh = turn(first * delay), turn(2 * delay)
         forms = [own]
         if n_d > 1:
-            by_yl = turn((8 - 16 * yl[0]) * delay)
+            by_4 = times(by_zh, by_zh)
+            by_8 = times(by_4, by_4)
+            by_yl = by_8[0], jnp.where(yl[0] == 0, by_8[1], -by_8[1])
             by_yh = turn((128 - 256 * yh[0]) * delay)
             other = times(own, by_yh)
             forms = [own, times(own, by_yl), other, times(other, by_yl)]
-        by_zh = turn(2 * delay)
         for d, value in enumerate(forms):
             for j in range(N_ZH):
                 if j > 0:
@@ -197,13 +198,27 @@
     return res[:NP] + jnp.where(left, cross, -cross)
 
 
-def slant_a_body(n_after, zh, base, yh, yl, slowness, places, data, *rest):
-    outs, (slow, high, low) = rest[n_after : n_after + N_ZH], rest[n_after + N_ZH :]
+def phase_a_body(base, yh, yl, slowness, places, high, low, slow):
     for parity in range(2):
         for place in range(2):
             row = 2 * place + parity
             positions = places[row : row + 1, :].astype(jnp.int32)
             phase_tables(1, base, yh, yl, slowness, positions, (2 * parity + place) * 128, slow, high, low)
+
+
+def phase_a(base, yh, yl, slowness, places):
+    return pl.pallas_call(
+        phase_a_body,
+        in_specs=[SCALAR] * 3 + [WHOLE] * 2,
+        out_specs=[WHOLE] * 2,
+        out_shape=[jax.ShapeDtypeStruct((N_ZH, 2 * NP, 512), jnp.bfloat16)] * 2,
+        scratch_shapes=[pltpu.VMEM((NP, 128), jnp.int32)],
+        name="phase_a",
+        **params(1 << 24, 2 << 20),
+    )(base, yh, yl, slowness, places)
+
+
+def slant_a_body(zh, high, low, data, *outs):
     for e, out in enumerate(outs):
         j = (zh[0] + e) & (N_ZH - 1)
         cols = []
@@ -213,16 +228,15 @@
         out[...] = stack(high[j], low[j], *cols)
 
 
-def slant_a(zh, base, yh, yl, slowness, places, data, after=()):
-    return pl.pallas_call(
-        functools.partial(slant_a_body, len(after)),
-        in_specs=[SCALAR] * 4 + [WHOLE] * 3 + [ANY] * len(after),
+def slant_a(zh, high, low, data):
+    return pl.pallas_call(
+        slant_a_body,
+        in_specs=[SCALAR] + [WHOLE] * 3,
         out_specs=[WHOLE] * N_ZH,
         out_shape=[jax.ShapeDtypeStruct((NP, 128), jnp.float32)] * N_ZH,
-        scratch_shapes=[pltpu.VMEM((NP, 128), jnp.int32)] + [pltpu.VMEM((N_ZH, 2 * NP, 512), jnp.bfloat16)] * 2,
         name="slant_a",
         **params(1 << 30, 5 << 20),
-    )(zh, base, yh, yl, slowness, places, data.reshape(N_XZ, 2 * PAIRS * 8, 128), *after)
+    )(zh, high, low, data.reshape(N_XZ, 2 * PAIRS * 8, 128))
 
 
 def slant_b_body(n_after, base, yh, yl, slowness, data, *rest):
@@ -326,7 +340,7 @@
     where = one(FREQ0 + c * 64 + x * 16 + zl), one(yh), one(yl), slowness.reshape(1, NP)
     *part_b, places = slant_b(*where, data_b, after=[both_a])
     part_b = exchange_y(part_b)
-    part_a = slant_a(one(zh), *where, places, data_a)
+    part_a = slant_a(one(zh), *phase_a(*where, places), data_a)
     part_b = sum_b(one(zh), part_b, after=[part_a[0]])
     return finish([*exchange_z(part_a), *exchange_z(part_b)])
 

time: 98.7 us -> 97.6 us (0.989)
  waiting for transfers between devices: 35.4 us -> 32.9 us
  local copies, waits for them, and re-layouts: 2.05 us -> 3.59 us
    all_to_all x1, waiting for transfers between devices: 4.19 us -> 1.72 us  [body(): data_a = lax.all_to_all(both_a, ('x', 'zl'), 0, 0, tiled=True)]
    unnamed x8 -> x12, local copies, waits for them, and re-layouts: 1.64 us -> 3.19 us
    pallas_call x1 -> x2, Pallas kernels: 2.8 us -> 2.63 us  [the longest x1 1.74 us: phase_a(): pl.pallas_call(phase_a_body, in_specs=[SCALAR] * 3 + [WHOLE] * 2, out_spe...]
  transfers between devices with their start and end apart: 17 -> 17, of which waited for: 6 -> 7; matrix products, arithmetic and copies ran while one was open for 0% -> 0% of each run, Pallas kernels for 16% -> 16%
where the time goes in v4:
time: 97.6 us; the launch traced here: 97.3 us
  starting transfers between devices  35.5 us (36%)
  waiting for transfers between devices  32.9 us (34%)
  Pallas kernels  25.2 us (26%)
  local copies, waits for them, and re-layouts  3.59 us (4%)
    ppermute x9, waiting for transfers between devices, swap(): return lax.ppermute(value, axes, [(i, i ^ mask) for i in range(size)])  24.1 us
    pallas_call x4, Pallas kernels, dft(): pl.pallas_call(functools.partial(body, len(after)), grid_spec=pltpu.Prefe...  16.3 us
    ppermute x6, starting transfers between devices, exchange_z(): lax.ppermute(parts[e], 'zh', shift(e))  14 us
    ppermute x9, starting transfers between devices, swap(): return lax.ppermute(value, axes, [(i, i ^ mask) for i in range(size)])  10.4 us
    ppermute x6, waiting for transfers between devices, exchange_z(): lax.ppermute(parts[e], 'zh', shift(e))  7.07 us
    all_to_all x1, starting transfers between devices, body(): data_b = lax.all_to_all(mine_b, ('x', 'zl'), 0, 0, tiled=True)  5.65 us
    all_to_all x1, starting transfers between devices, body(): data_a = lax.all_to_all(both_a, ('x', 'zl'), 0, 0, tiled=True)  5.42 us
    pallas_call x1, Pallas kernels, slant_b(): pl.pallas_call(functools.partial(slant_b_body, len(after)), in_specs=[SCA...  4.37 us
  transfers between devices with their start and end apart: 17, of which 7 were waited for; matrix products, arithmetic and copies ran while one was open for 0% of the time, Pallas kernels for 16%

profile of v4, /device:TPU:64, one launch (start us, length us, event | category | flops | bytes accessed | tf_op | source)
XLA Modules:
  0.0 97.3 jit_solution(12904345414103445470)
XLA Ops:
  0.0 4.2 %other_a.1.rest_0_ = f32[4,8,16,8,128]{4,3,2,1,0:T(8,128)} custom-call(s32[1]{0:T(128)} %bitcast.5.index, bf16[8,2,256,1024]{3,2,1,0:T(8,128)(2,1)} %constant.36.clone.table, bf16[32,128,1024]{2,1,0:T(8,128)(2,1)} %traces.7), custom_call_target="tpu_custom_call" | custom-call | flops 1073741824 | bytes 7340032 | tf_op jit(solution)/shard_map/other_a/pallas_call | solution.py:101
  4.2 0.0 copy-start.5
  4.2 0.0 collective-permute-start.2
  4.2 3.3 %other_b.1.rest_0_ = f32[4,8,16,8,128]{4,3,2,1,0:T(8,128)S(1)} custom-call(s32[1]{0:T(128)} %bitcast.5.index, bf16[8,2,256,1024]{3,2,1,0:T(8,128)(2,1)} %constant.36.clone.table, bf16[32,128,1024]{2,1,0:T(8,128)(2,1)} %traces.7, f32[4,8,16,8,128]{4,3,2,1,0:T(8,128)} %other_a.1.rest_0_), custom_call_target="tpu_custom_call" | custom-call | flops 1073741824 | bytes 7340032 | tf_op jit(solution)/shard_map/other_b/pallas_call | solution.py:101
  7.5 0.6 collective-permute-start
  8.1 0.1 mul.45
  8.1 0.1 mul.46
  8.2 0.0 copy-done.5
  8.2 0.1 mul.41
  8.3 0.1 copy.6
  8.4 0.1 mul.43
  8.5 1.7 %collective-permute-start.1 = (f32[8,128]{1,0:T(8,128)S(1)}, f32[8,128]{1,0:T(8,128)S(1)}, u32[]{:S(2)}, u32[]{:S(2)}) collective-permute-start(f32[8,128]{1,0:T(8,128)S(1)} %pad.4.here), channel_id=1, source_target_pairs={{0,8},{8,0},{1,9},{9,1},{2,10},{10,2},{3,11},{11,3},{4,12},{12,4},... | collective-permute-start | bytes 12296 | tf_op jit(solution)/shard_map/ppermute | solution.py:309
  10.2 0.0 collective-permute-done.2.other
  10.2 3.8 %mine_a.1 = (f32[8,16,8,128]{3,2,1,0:T(8,128)S(1)}, f32[8,16,8,128]{3,2,1,0:T(8,128)S(1)}, f32[8,16,8,128]{3,2,1,0:T(8,128)S(1)}, f32[8,16,8,128]{3,2,1,0:T(8,128)S(1)}) custom-call(s32[1]{0:T(128)} %bitcast.5.index, bf16[8,2,256,1024]{3,2,1,0:T(8,128)(2,1)} %constant.36.clone.table, bf16[32,128,1024]{2,1,0:T(8,128)(2,1)} %traces.7, ...), custom_call_target="tpu_custom_call" | custom-call | flops 1073741824 | bytes 7340032 | tf_op jit(solution)/shard_map/mine_a/pallas_call | solution.py:101
  14.0 0.0 copy-start
  14.0 0.0 copy-start.1
  14.0 0.0 collective-permute-done.1.there
  14.0 0.0 collective-permute-done.other
  14.0 0.8 copy-done
  14.8 0.2 copy-done.1
  15.0 5.0 %mine_b.1.rest_0_ = f32[8,65,8,128]{3,2,1,0:T(8,128)} custom-call(s32[1]{0:T(128)} %bitcast.5.index, bf16[8,2,256,1024]{3,2,1,0:T(8,128)(2,1)} %constant.36.clone.table, bf16[32,128,1024]{2,1,0:T(8,128)(2,1)} %traces.7, f32[4,8,16,8,128]{4,3,2,1,0:T(8,128)} %collective-permute-done.other, f32[8,128]{1,0:T(8,128)S(1)} %pad.4.here, ...), custom_call_target="tpu_custom_call" | custom-call | flops 1073741824 | bytes 7340032 | tf_op jit(solution)/shard_map/mine_b/pallas_call | solution.py:101
  20.0 5.7 %all-to-all-start = ((f32[8,65,8,128]{3,2,1,0:T(8,128)}), f32[8,65,8,128]{3,2,1,0:T(8,128)S(1)}, u32[]{:S(2)}, u32[]{:S(2)}) async-start(f32[8,65,8,128]{3,2,1,0:T(8,128)} %mine_b.1.rest_0_), calls=%async_computation | async-start | bytes 4259840 | tf_op jit(solution)/shard_map/all_to_all | solution.py:336
  25.7 0.4 collective-permute-start.3
  26.1 3.2 %collective-permute-start.4 = (f32[8,16,8,128]{3,2,1,0:T(8,128)}, f32[8,16,8,128]{3,2,1,0:T(8,128)S(1)}, u32[]{:S(2)}, u32[]{:S(2)}) collective-permute-start(f32[8,16,8,128]{3,2,1,0:T(8,128)} %copy-done), channel_id=1, source_target_pairs={{0,128},{8,136},{128,0},{136,8},{1,129},{9,137},{129,1},{137,9},{2... | collective-permute-start | bytes 1572872 | tf_op jit(solution)/shard_map/ppermute | solution.py:309
  29.3 0.0 copy-start.2
  29.3 1.1 %collective-permute-start.5 = (f32[8,16,8,128]{3,2,1,0:T(8,128)S(1)}, f32[8,16,8,128]{3,2,1,0:T(8,128)S(1)}, u32[]{:S(2)}, u32[]{:S(2)}) collective-permute-start(f32[8,16,8,128]{3,2,1,0:T(8,128)S(1)} %get-tuple-element.27), channel_id=1, source_target_pairs={{0,136},{8,128},{128,8},{136,0},{1,137},{9,129},{129,9},{137,1},{2... | collective-permute-start | bytes 1572872 | tf_op jit(solution)/shard_map/ppermute | solution.py:309
  30.4 10.4 %collective-permute-done.3.yl = f32[8,16,8,128]{3,2,1,0:T(8,128)S(1)} collective-permute-done((f32[8,16,8,128]{3,2,1,0:T(8,128)}, f32[8,16,8,128]{3,2,1,0:T(8,128)S(1)}, u32[]{:S(2)}, u32[]{:S(2)}) %collective-permute-start.3) | collective-permute-done | bytes 524320 | tf_op jit(solution)/shard_map/ppermute | solution.py:309
  40.7 11.4 %collective-permute-done.4.yh = f32[8,16,8,128]{3,2,1,0:T(8,128)S(1)} collective-permute-done((f32[8,16,8,128]{3,2,1,0:T(8,128)}, f32[8,16,8,128]{3,2,1,0:T(8,128)S(1)}, u32[]{:S(2)}, u32[]{:S(2)}) %collective-permute-start.4) | collective-permute-done | bytes 524320 | tf_op jit(solution)/shard_map/ppermute | solution.py:309
  52.1 2.4 %collective-permute-done.5.both = f32[8,16,8,128]{3,2,1,0:T(8,128)S(1)} collective-permute-done((f32[8,16,8,128]{3,2,1,0:T(8,128)S(1)}, f32[8,16,8,128]{3,2,1,0:T(8,128)S(1)}, u32[]{:S(2)}, u32[]{:S(2)}) %collective-permute-start.5) | collective-permute-done | bytes 524320 | tf_op jit(solution)/shard_map/ppermute | solution.py:309
  54.5 1.1 %sum_a.1.rest_0_ = f32[8,2,16,8,128]{4,3,2,1,0:T(8,128)} custom-call(f32[8,16,8,128]{3,2,1,0:T(8,128)S(1)} %get-tuple-element.24.rest_0_.own, f32[8,16,8,128]{3,2,1,0:T(8,128)S(1)} %collective-permute-done.3.yl, f32[8,16,8,128]{3,2,1,0:T(8,128)S(1)} %collective-permute-done.4.yh, f32[8,16,8,128]{3,2,1,0:T(8,128)S(1)} %collective-permute-done.5.both, ...), custom_call_target="tpu_custom_call" | custom-call | flops 262144 | bytes 3145728 | tf_op jit(solution)/shard_map/sum_a/pallas_call | solution.py:128
  55.6 0.0 all-to-all-done
  55.6 5.4 %all-to-all-start.1 = ((f32[8,2,16,8,128]{4,3,2,1,0:T(8,128)}), f32[8,2,16,8,128]{4,3,2,1,0:T(8,128)S(1)}, u32[]{:S(2)}, u32[]{:S(2)}) async-start(f32[8,2,16,8,128]{4,3,2,1,0:T(8,128)} %sum_a.1.rest_0_), calls=%async_computation.1 | async-start | bytes 2097152 | tf_op jit(solution)/shard_map/all_to_all | solution.py:338
  61.0 0.0 copy-done.2
  61.0 4.4 %slant_b.1 = (f32[4,128,128]{2,1,0:T(8,128)S(1)}, f32[4,128,128]{2,1,0:T(8,128)}, f32[4,128,128]{2,1,0:T(8,128)}, f32[4,128,128]{2,1,0:T(8,128)}, f32[8,128]{1,0:T(8,128)S(1)}) custom-call(s32[1]{0:T(128)} %bitcast.1.base, s32[1]{0:T(128)} %bitcast.2.yh, s32[1]{0:T(128)} %bitcast.3.yl, s32[1,128]{1,0:T(1,128)S(1)} %bitcast.14, f32[8,520,128]{2,1,0:T(8,128)S(1)} %bitcast.12, ...), custom_call_target="tpu_custom_call" | custom-call | flops 2147483648 | bytes 7340032 | tf_op jit(solution)/shard_map/slant_b/pallas_call | solution.py:259
  65.4 0.0 collective-permute-start.10
  65.4 2.1 %collective-permute-start.11 = (f32[4,128,128]{2,1,0:T(8,128)}, f32[4,128,128]{2,1,0:T(8,128)S(1)}, u32[]{:S(2)}, u32[]{:S(2)}) collective-permute-start(f32[4,128,128]{2,1,0:T(8,128)} %get-tuple-element.38), channel_id=1, source_target_pairs={{0,136},{8,128},{128,8},{136,0},{1,137},{9,129},{129,9},{137,1},{2... | collective-permute-start | bytes 786440 | tf_op jit(solution)/shard_map/ppermute | solution.py:309
  67.5 1.3 %collective-permute-start.9 = (f32[4,128,128]{2,1,0:T(8,128)}, f32[4,128,128]{2,1,0:T(8,128)S(1)}, u32[]{:S(2)}, u32[]{:S(2)}) collective-permute-start(f32[4,128,128]{2,1,0:T(8,128)} %get-tuple-element.36), channel_id=1, source_target_pairs={{0,8},{8,0},{128,136},{136,128},{1,9},{9,1},{129,137},{137,129},{2... | collective-permute-start | bytes 786440 | tf_op jit(solution)/shard_map/ppermute | solution.py:309
  68.9 1.7 %phase_a.1 = (bf16[4,256,512]{2,1,0:T(8,128)(2,1)S(1)}, bf16[4,256,512]{2,1,0:T(8,128)(2,1)S(1)}) custom-call(s32[1]{0:T(128)} %bitcast.1.base, s32[1]{0:T(128)} %bitcast.2.yh, s32[1]{0:T(128)} %bitcast.3.yl, s32[1,128]{1,0:T(1,128)S(1)} %bitcast.15, f32[8,128]{1,0:T(8,128)S(1)} %get-tuple-element.28.places), custom_call_target="tpu_custom_call" | custom-call | flops 16777216 | bytes 2097152 | tf_op jit(solution)/shard_map/phase_a/pallas_call | solution.py:210
  70.6 0.0 copy-start.3
  70.6 1.0 copy-done.3
  71.6 1.7 %all-to-all-done.1 = f32[8,2,16,8,128]{4,3,2,1,0:T(8,128)S(1)} async-done(((f32[8,2,16,8,128]{4,3,2,1,0:T(8,128)}), f32[8,2,16,8,128]{4,3,2,1,0:T(8,128)S(1)}, u32[]{:S(2)}, u32[]{:S(2)}) %all-to-all-start.1) | async-done | bytes 1048608 | tf_op jit(solution)/shard_map/all_to_all | solution.py:338
  73.3 0.0 copy-start.4
  73.3 1.2 %copy-done.4 = bf16[4,256,512]{2,1,0:T(8,128)(2,1)S(1)} copy-done((bf16[4,256,512]{2,1,0:T(8,128)(2,1)S(1)}, bf16[4,256,512]{2,1,0:T(8,128)(2,1)}, u32[]{:S(2)}) %copy-start.4) | copy-done | bytes 1048600
  74.5 0.9 slant_a.1
  75.4 3.8 %collective-permute-start.6 = (f32[128,128]{1,0:T(8,128)S(1)}, f32[128,128]{1,0:T(8,128)S(1)}, u32[]{:S(2)}, u32[]{:S(2)}) collective-permute-start(f32[128,128]{1,0:T(8,128)S(1)} %get-tuple-element.32), channel_id=1, source_target_pairs={{0,2},{2,4},{4,6},{6,0},{1,3},{3,5},{5,7},{7,1},{8,10},{10,12},{12... | collective-permute-start | bytes 196616 | tf_op jit(solution)/shard_map/ppermute | solution.py:318
  79.3 1.0 %collective-permute-start.7 = (f32[128,128]{1,0:T(8,128)S(1)}, f32[128,128]{1,0:T(8,128)S(1)}, u32[]{:S(2)}, u32[]{:S(2)}) collective-permute-start(f32[128,128]{1,0:T(8,128)S(1)} %get-tuple-element.33), channel_id=1, source_target_pairs={{0,4},{2,6},{4,0},{6,2},{1,5},{3,7},{5,1},{7,3},{8,12},{10,14},{12... | collective-permute-start | bytes 196616 | tf_op jit(solution)/shard_map/ppermute | solution.py:318
  80.3 0.0 collective-permute-done.10.yh
  80.3 2.8 %collective-permute-start.8 = (f32[128,128]{1,0:T(8,128)S(1)}, f32[128,128]{1,0:T(8,128)S(1)}, u32[]{:S(2)}, u32[]{:S(2)}) collective-permute-start(f32[128,128]{1,0:T(8,128)S(1)} %get-tuple-element.34), channel_id=1, source_target_pairs={{0,6},{2,0},{4,2},{6,4},{1,7},{3,1},{5,3},{7,5},{8,14},{10,8},{12,... | collective-permute-start | bytes 196616 | tf_op jit(solution)/shard_map/ppermute | solution.py:318
  83.1 0.0 collective-permute-done.11.both
  83.1 0.0 collective-permute-done.9.yl
  83.1 0.1 sum_b.1
  83.2 1.4 %collective-permute-start.12 = (f32[128,128]{1,0:T(8,128)S(1)}, f32[128,128]{1,0:T(8,128)S(1)}, u32[]{:S(2)}, u32[]{:S(2)}) collective-permute-start(f32[128,128]{1,0:T(8,128)S(1)} %get-tuple-element.40), channel_id=1, source_target_pairs={{0,2},{2,4},{4,6},{6,0},{1,3},{3,5},{5,7},{7,1},{8,10},{10,12},{12... | collective-permute-start | bytes 196616 | tf_op jit(solution)/shard_map/ppermute | solution.py:318
  84.6 4.9 %collective-permute-start.13 = (f32[128,128]{1,0:T(8,128)S(1)}, f32[128,128]{1,0:T(8,128)S(1)}, u32[]{:S(2)}, u32[]{:S(2)}) collective-permute-start(f32[128,128]{1,0:T(8,128)S(1)} %get-tuple-element.41), channel_id=1, source_target_pairs={{0,4},{2,6},{4,0},{6,2},{1,5},{3,7},{5,1},{7,3},{8,12},{10,14},{12... | collective-permute-start | bytes 196616 | tf_op jit(solution)/shard_map/ppermute | solution.py:318
  89.5 0.0 collective-permute-done.6.refs_1_
  89.5 0.0 collective-permute-start.14
  89.5 0.0 collective-permute-done.7.refs_2_
  89.5 0.4 collective-permute-done.8.refs_3_
  89.9 0.0 collective-permute-done.12.refs_5_
  89.9 2.8 %collective-permute-done.13.refs_6_ = f32[128,128]{1,0:T(8,128)S(1)} collective-permute-done((f32[128,128]{1,0:T(8,128)S(1)}, f32[128,128]{1,0:T(8,128)S(1)}, u32[]{:S(2)}, u32[]{:S(2)}) %collective-permute-start.13) | collective-permute-done | bytes 65568 | tf_op jit(solution)/shard_map/ppermute | solution.py:318
  92.7 3.8 %collective-permute-done.14.refs_7_ = f32[128,128]{1,0:T(8,128)S(1)} collective-permute-done((f32[128,128]{1,0:T(8,128)S(1)}, f32[128,128]{1,0:T(8,128)S(1)}, u32[]{:S(2)}, u32[]{:S(2)}) %collective-permute-start.14) | collective-permute-done | bytes 65568 | tf_op jit(solution)/shard_map/ppermute | solution.py:318
  96.6 0.8 finish.1
  (4 shorter events, 0.0 us)
Async XLA Ops:
  4.2 4.1 %copy-start.5 = (s32[32]{0:T(128)S(1)}, s32[32]{0:T(128)}, u32[]{:S(2)}) copy-start(s32[32]{0:T(128)} %param.5) | copy-start | bytes 388
  4.2 6.0 %collective-permute-start.2 = (f32[4,8,16,8,128]{4,3,2,1,0:T(8,128)}, f32[4,8,16,8,128]{4,3,2,1,0:T(8,128)}, u32[]{:S(2)}, u32[]{:S(2)}) collective-permute-start(f32[4,8,16,8,128]{4,3,2,1,0:T(8,128)} %other_a.1.rest_0_), channel_id=1, source_target_pairs={{0,64},{64,0},{1,65},{65,1},{2,66},{66,2},{3,67},{67,3},{4,68},{68... | collective-permute-start | bytes 6291464 | tf_op jit(solution)/shard_map/ppermute | solution.py:309
  7.5 6.5 %collective-permute-start = (f32[4,8,16,8,128]{4,3,2,1,0:T(8,128)S(1)}, f32[4,8,16,8,128]{4,3,2,1,0:T(8,128)}, u32[]{:S(2)}, u32[]{:S(2)}) collective-permute-start(f32[4,8,16,8,128]{4,3,2,1,0:T(8,128)S(1)} %other_b.1.rest_0_), channel_id=1, source_target_pairs={{0,64},{64,0},{1,65},{65,1},{2,66},{66,2},{3,67},{67,3},{4,68},{68... | collective-permute-start | bytes 6291464 | tf_op jit(solution)/shard_map/ppermute | solution.py:309
  8.5 5.5 %collective-permute-start.1 = (f32[8,128]{1,0:T(8,128)S(1)}, f32[8,128]{1,0:T(8,128)S(1)}, u32[]{:S(2)}, u32[]{:S(2)}) collective-permute-start(f32[8,128]{1,0:T(8,128)S(1)} %pad.4.here), channel_id=1, source_target_pairs={{0,8},{8,0},{1,9},{9,1},{2,10},{10,2},{3,11},{11,3},{4,12},{12,4},... | collective-permute-start | bytes 12296 | tf_op jit(solution)/shard_map/ppermute | solution.py:309
  14.0 0.8 copy-start
  14.0 1.0 %copy-start.1 = (f32[8,16,8,128]{3,2,1,0:T(8,128)}, f32[8,16,8,128]{3,2,1,0:T(8,128)S(1)}, u32[]{:S(2)}) copy-start(f32[8,16,8,128]{3,2,1,0:T(8,128)S(1)} %get-tuple-element.25) | copy-start | bytes 1572868
  20.0 35.6 %all-to-all-start = ((f32[8,65,8,128]{3,2,1,0:T(8,128)}), f32[8,65,8,128]{3,2,1,0:T(8,128)S(1)}, u32[]{:S(2)}, u32[]{:S(2)}) async-start(f32[8,65,8,128]{3,2,1,0:T(8,128)} %mine_b.1.rest_0_), calls=%async_computation | async-start | bytes 4259840 | tf_op jit(solution)/shard_map/all_to_all | solution.py:336
  25.7 15.1 %collective-permute-start.3 = (f32[8,16,8,128]{3,2,1,0:T(8,128)}, f32[8,16,8,128]{3,2,1,0:T(8,128)S(1)}, u32[]{:S(2)}, u32[]{:S(2)}) collective-permute-start(f32[8,16,8,128]{3,2,1,0:T(8,128)} %copy-done.1), channel_id=1, source_target_pairs={{0,8},{8,0},{128,136},{136,128},{1,9},{9,1},{129,137},{137,129},{2... | collective-permute-start | bytes 1572872 | tf_op jit(solution)/shard_map/ppermute | solution.py:309
  26.1 26.0 %collective-permute-start.4 = (f32[8,16,8,128]{3,2,1,0:T(8,128)}, f32[8,16,8,128]{3,2,1,0:T(8,128)S(1)}, u32[]{:S(2)}, u32[]{:S(2)}) collective-permute-start(f32[8,16,8,128]{3,2,1,0:T(8,128)} %copy-done), channel_id=1, source_target_pairs={{0,128},{8,136},{128,0},{136,8},{1,129},{9,137},{129,1},{137,9},{2... | collective-permute-start | bytes 1572872 | tf_op jit(solution)/shard_map/ppermute | solution.py:309
  29.3 31.7 %copy-start.2 = (s32[128]{0:T(128)S(1)}, s32[128]{0:T(128)}, u32[]{:S(2)}) copy-start(s32[128]{0:T(128)} %param.6) | copy-start | bytes 1540
  29.3 25.2 %collective-permute-start.5 = (f32[8,16,8,128]{3,2,1,0:T(8,128)S(1)}, f32[8,16,8,128]{3,2,1,0:T(8,128)S(1)}, u32[]{:S(2)}, u32[]{:S(2)}) collective-permute-start(f32[8,16,8,128]{3,2,1,0:T(8,128)S(1)} %get-tuple-element.27), channel_id=1, source_target_pairs={{0,136},{8,128},{128,8},{136,0},{1,137},{9,129},{129,9},{137,1},{2... | collective-permute-start | bytes 1572872 | tf_op jit(solution)/shard_map/ppermute | solution.py:309
  55.6 17.7 %all-to-all-start.1 = ((f32[8,2,16,8,128]{4,3,2,1,0:T(8,128)}), f32[8,2,16,8,128]{4,3,2,1,0:T(8,128)S(1)}, u32[]{:S(2)}, u32[]{:S(2)}) async-start(f32[8,2,16,8,128]{4,3,2,1,0:T(8,128)} %sum_a.1.rest_0_), calls=%async_computation.1 | async-start | bytes 2097152 | tf_op jit(solution)/shard_map/all_to_all | solution.py:338
  65.4 14.9 %collective-permute-start.10 = (f32[4,128,128]{2,1,0:T(8,128)}, f32[4,128,128]{2,1,0:T(8,128)S(1)}, u32[]{:S(2)}, u32[]{:S(2)}) collective-permute-start(f32[4,128,128]{2,1,0:T(8,128)} %get-tuple-element.37), channel_id=1, source_target_pairs={{0,128},{8,136},{128,0},{136,8},{1,129},{9,137},{129,1},{137,9},{2... | collective-permute-start | bytes 786440 | tf_op jit(solution)/shard_map/ppermute | solution.py:309
  65.4 17.7 %collective-permute-start.11 = (f32[4,128,128]{2,1,0:T(8,128)}, f32[4,128,128]{2,1,0:T(8,128)S(1)}, u32[]{:S(2)}, u32[]{:S(2)}) collective-permute-start(f32[4,128,128]{2,1,0:T(8,128)} %get-tuple-element.38), channel_id=1, source_target_pairs={{0,136},{8,128},{128,8},{136,0},{1,137},{9,129},{129,9},{137,1},{2... | collective-permute-start | bytes 786440 | tf_op jit(solution)/shard_map/ppermute | solution.py:309
  67.5 15.6 %collective-permute-start.9 = (f32[4,128,128]{2,1,0:T(8,128)}, f32[4,128,128]{2,1,0:T(8,128)S(1)}, u32[]{:S(2)}, u32[]{:S(2)}) collective-permute-start(f32[4,128,128]{2,1,0:T(8,128)} %get-tuple-element.36), channel_id=1, source_target_pairs={{0,8},{8,0},{128,136},{136,128},{1,9},{9,1},{129,137},{137,129},{2... | collective-permute-start | bytes 786440 | tf_op jit(solution)/shard_map/ppermute | solution.py:309
  70.6 1.0 copy-start.3
  73.3 1.2 %copy-start.4 = (bf16[4,256,512]{2,1,0:T(8,128)(2,1)S(1)}, bf16[4,256,512]{2,1,0:T(8,128)(2,1)}, u32[]{:S(2)}) copy-start(bf16[4,256,512]{2,1,0:T(8,128)(2,1)} %copy-done.3) | copy-start | bytes 3145732
  75.4 14.0 %collective-permute-start.6 = (f32[128,128]{1,0:T(8,128)S(1)}, f32[128,128]{1,0:T(8,128)S(1)}, u32[]{:S(2)}, u32[]{:S(2)}) collective-permute-start(f32[128,128]{1,0:T(8,128)S(1)} %get-tuple-element.32), channel_id=1, source_target_pairs={{0,2},{2,4},{4,6},{6,0},{1,3},{3,5},{5,7},{7,1},{8,10},{10,12},{12... | collective-permute-start | bytes 196616 | tf_op jit(solution)/shard_map/ppermute | solution.py:318
  79.3 10.2 %collective-permute-start.7 = (f32[128,128]{1,0:T(8,128)S(1)}, f32[128,128]{1,0:T(8,128)S(1)}, u32[]{:S(2)}, u32[]{:S(2)}) collective-permute-start(f32[128,128]{1,0:T(8,128)S(1)} %get-tuple-element.33), channel_id=1, source_target_pairs={{0,4},{2,6},{4,0},{6,2},{1,5},{3,7},{5,1},{7,3},{8,12},{10,14},{12... | collective-permute-start | bytes 196616 | tf_op jit(solution)/shard_map/ppermute | solution.py:318
  80.3 9.7 %collective-permute-start.8 = (f32[128,128]{1,0:T(8,128)S(1)}, f32[128,128]{1,0:T(8,128)S(1)}, u32[]{:S(2)}, u32[]{:S(2)}) collective-permute-start(f32[128,128]{1,0:T(8,128)S(1)} %get-tuple-element.34), channel_id=1, source_target_pairs={{0,6},{2,0},{4,2},{6,4},{1,7},{3,1},{5,3},{7,5},{8,14},{10,8},{12,... | collective-permute-start | bytes 196616 | tf_op jit(solution)/shard_map/ppermute | solution.py:318
  83.2 6.8 %collective-permute-start.12 = (f32[128,128]{1,0:T(8,128)S(1)}, f32[128,128]{1,0:T(8,128)S(1)}, u32[]{:S(2)}, u32[]{:S(2)}) collective-permute-start(f32[128,128]{1,0:T(8,128)S(1)} %get-tuple-element.40), channel_id=1, source_target_pairs={{0,2},{2,4},{4,6},{6,0},{1,3},{3,5},{5,7},{7,1},{8,10},{10,12},{12... | collective-permute-start | bytes 196616 | tf_op jit(solution)/shard_map/ppermute | solution.py:318
  84.6 8.2 %collective-permute-start.13 = (f32[128,128]{1,0:T(8,128)S(1)}, f32[128,128]{1,0:T(8,128)S(1)}, u32[]{:S(2)}, u32[]{:S(2)}) collective-permute-start(f32[128,128]{1,0:T(8,128)S(1)} %get-tuple-element.41), channel_id=1, source_target_pairs={{0,4},{2,6},{4,0},{6,2},{1,5},{3,7},{5,1},{7,3},{8,12},{10,14},{12... | collective-permute-start | bytes 196616 | tf_op jit(solution)/shard_map/ppermute | solution.py:318
  89.5 7.1 %collective-permute-start.14 = (f32[128,128]{1,0:T(8,128)S(1)}, f32[128,128]{1,0:T(8,128)S(1)}, u32[]{:S(2)}, u32[]{:S(2)}) collective-permute-start(f32[128,128]{1,0:T(8,128)S(1)} %get-tuple-element.42), channel_id=1, source_target_pairs={{0,6},{2,0},{4,2},{6,4},{1,7},{3,1},{5,3},{7,5},{8,14},{10,8},{12,... | collective-permute-start | bytes 196616 | tf_op jit(solution)/shard_map/ppermute | solution.py:318

commit v5 on v4

--- a/solution.py
+++ b/solution.py
@@ -268,28 +268,29 @@
 
 
 def sum_b_body(zh, own, yl, yh, both, *rest):
-    outs = rest[-N_ZH:]
+    halves, outs = rest[:N_ZH], rest[N_ZH:]
     for e, out in enumerate(outs):
         j = (zh[0] + e) & (N_ZH - 1)
-        out[...] = (own[j] + yl[j]) + (yh[j] + both[j])
-
-
-def sum_b(zh, parts, after=()):
+        out[0] = halves[e][...]
+        out[1] = (own[j] + yl[j]) + (yh[j] + both[j])
+
+
+def sum_b(zh, parts, halves):
     return pl.pallas_call(
         sum_b_body,
-        in_specs=[SCALAR] + [WHOLE] * N_Y + [ANY] * len(after),
+        in_specs=[SCALAR] + [WHOLE] * (N_Y + N_ZH),
         out_specs=[WHOLE] * N_ZH,
-        out_shape=[jax.ShapeDtypeStruct((NP, 128), jnp.float32)] * N_ZH,
+        out_shape=[jax.ShapeDtypeStruct((2, NP, 128), jnp.float32)] * N_ZH,
         name="sum_b",
         **params(1 << 18, 1 << 20),
-    )(zh, *parts, *after)
-
-
-def finish_body(*refs):
+    )(zh, *parts, *halves)
+
+
+def finish_body(own, *rest):
     scale = jnp.float32(1.0 / math.sqrt(NT) / math.sqrt(SHOTS))
     left = lax.broadcasted_iota(jnp.int32, (NP, 128), 1) < HALF
-    total = lambda four: ((four[0][...] + four[1][...]) + (four[2][...] + four[3][...])) * scale
-    a, b, out = total(refs[:4]), total(refs[4:8]), refs[8]
+    out = rest[-1]
+    a, b = (((own[i] + rest[0][i]) + (rest[1][i] + rest[2][i])) * scale for i in range(2))
     out[0, 0] = jnp.where(left, a, pltpu.roll(b, HALF, 1))
     out[0, 1] = jnp.where(left, pltpu.roll(a, HALF, 1), b)
 
@@ -297,7 +298,7 @@
 def finish(parts):
     return pl.pallas_call(
         finish_body,
-        in_specs=[WHOLE] * 8,
+        in_specs=[WHOLE] * N_ZH,
         out_specs=WHOLE,
         out_shape=jax.ShapeDtypeStruct((1, 2, NP, REC), jnp.float32),
         name="finish",
@@ -341,8 +342,7 @@
     *part_b, places = slant_b(*where, data_b, after=[both_a])
     part_b = exchange_y(part_b)
     part_a = slant_a(one(zh), *phase_a(*where, places), data_a)
-    part_b = sum_b(one(zh), part_b, after=[part_a[0]])
-    return finish([*exchange_z(part_a), *exchange_z(part_b)])
+    return finish(exchange_z(sum_b(one(zh), part_b, part_a)))
 
 
 def solution(mesh):

time: 97.6 us -> 95.1 us (0.974); the launches traced: 97.3 us -> 93.5 us
  starting transfers between devices: 35.5 us -> 31.4 us
    ppermute x6 -> x3, starting transfers between devices: 14 us -> 8.72 us  [exchange_z(): lax.ppermute(parts[e], 'zh', shift(e))]
    ppermute x9, waiting for transfers between devices: 24.1 us -> 27.4 us  [swap(): return lax.ppermute(value, axes, [(i, i ^ mask) for i in range(size)])]
    ppermute x6 -> x3, waiting for transfers between devices: 7.07 us -> 5.16 us  [exchange_z(): lax.ppermute(parts[e], 'zh', shift(e))]
    all_to_all x1, waiting for transfers between devices: 1.72 us -> 0.49 us  [body(): data_a = lax.all_to_all(both_a, ('x', 'zl'), 0, 0, tiled=True)]
    ppermute x9, starting transfers between devices: 10.4 us -> 11.7 us  [swap(): return lax.ppermute(value, axes, [(i, i ^ mask) for i in range(size)])]
  transfers between devices with their start and end apart: 17 -> 14, of which waited for: 7 -> 8; matrix products, arithmetic and copies ran while one was open for 0% -> 0% of each run, Pallas kernels for 16% -> 16%
where the time goes in v5:
time: 95.1 us; the launch traced here: 93.5 us
  waiting for transfers between devices  33.1 us (35%)
  starting transfers between devices  31.4 us (33%)
  Pallas kernels  25.3 us (27%)
  local copies, waits for them, and re-layouts  3.58 us (4%)
    ppermute x9, waiting for transfers between devices, swap(): return lax.ppermute(value, axes, [(i, i ^ mask) for i in range(size)])  27.4 us
    pallas_call x4, Pallas kernels, dft(): pl.pallas_call(functools.partial(body, len(after)), grid_spec=pltpu.Prefe...  16.3 us
    ppermute x9, starting transfers between devices, swap(): return lax.ppermute(value, axes, [(i, i ^ mask) for i in range(size)])  11.7 us
    ppermute x3, starting transfers between devices, exchange_z(): lax.ppermute(parts[e], 'zh', shift(e))  8.72 us
    all_to_all x1, starting transfers between devices, body(): data_b = lax.all_to_all(mine_b, ('x', 'zl'), 0, 0, tiled=True)  5.65 us
    all_to_all x1, starting transfers between devices, body(): data_a = lax.all_to_all(both_a, ('x', 'zl'), 0, 0, tiled=True)  5.42 us
    ppermute x3, waiting for transfers between devices, exchange_z(): lax.ppermute(parts[e], 'zh', shift(e))  5.16 us
    pallas_call x1, Pallas kernels, slant_b(): pl.pallas_call(functools.partial(slant_b_body, len(after)), in_specs=[SCA...  4.38 us
  transfers between devices with their start and end apart: 14, of which 8 were waited for; matrix products, arithmetic and copies ran while one was open for 0% of the time, Pallas kernels for 16%

profile of v5, /device:TPU:64, one launch (start us, length us, event | category | flops | bytes accessed | tf_op | source)
XLA Modules:
  0.0 93.5 jit_solution(11938630117179550644)
XLA Ops:
  0.0 4.2 %other_a.1.rest_0_ = f32[4,8,16,8,128]{4,3,2,1,0:T(8,128)} custom-call(s32[1]{0:T(128)} %bitcast.5.index, bf16[8,2,256,1024]{3,2,1,0:T(8,128)(2,1)} %constant.36.clone.table, bf16[32,128,1024]{2,1,0:T(8,128)(2,1)} %traces.7), custom_call_target="tpu_custom_call" | custom-call | flops 1073741824 | bytes 7340032 | tf_op jit(solution)/shard_map/other_a/pallas_call | solution.py:101
  4.2 0.0 copy-start.5
  4.2 0.0 collective-permute-start.2
  4.2 3.3 %other_b.1.rest_0_ = f32[4,8,16,8,128]{4,3,2,1,0:T(8,128)S(1)} custom-call(s32[1]{0:T(128)} %bitcast.5.index, bf16[8,2,256,1024]{3,2,1,0:T(8,128)(2,1)} %constant.36.clone.table, bf16[32,128,1024]{2,1,0:T(8,128)(2,1)} %traces.7, f32[4,8,16,8,128]{4,3,2,1,0:T(8,128)} %other_a.1.rest_0_), custom_call_target="tpu_custom_call" | custom-call | flops 1073741824 | bytes 7340032 | tf_op jit(solution)/shard_map/other_b/pallas_call | solution.py:101
  7.6 0.6 collective-permute-start
  8.2 0.1 mul.45
  8.2 0.1 mul.46
  8.3 0.0 copy-done.5
  8.3 0.1 mul.41
  8.4 0.1 copy.6
  8.5 0.1 mul.43
  8.6 1.7 %collective-permute-start.1 = (f32[8,128]{1,0:T(8,128)S(1)}, f32[8,128]{1,0:T(8,128)S(1)}, u32[]{:S(2)}, u32[]{:S(2)}) collective-permute-start(f32[8,128]{1,0:T(8,128)S(1)} %pad.4.here), channel_id=1, source_target_pairs={{0,8},{8,0},{1,9},{9,1},{2,10},{10,2},{3,11},{11,3},{4,12},{12,4},... | collective-permute-start | bytes 12296 | tf_op jit(solution)/shard_map/ppermute | solution.py:310
  10.3 0.0 collective-permute-done.2.other
  10.3 3.8 %mine_a.1 = (f32[8,16,8,128]{3,2,1,0:T(8,128)S(1)}, f32[8,16,8,128]{3,2,1,0:T(8,128)S(1)}, f32[8,16,8,128]{3,2,1,0:T(8,128)S(1)}, f32[8,16,8,128]{3,2,1,0:T(8,128)S(1)}) custom-call(s32[1]{0:T(128)} %bitcast.5.index, bf16[8,2,256,1024]{3,2,1,0:T(8,128)(2,1)} %constant.36.clone.table, bf16[32,128,1024]{2,1,0:T(8,128)(2,1)} %traces.7, ...), custom_call_target="tpu_custom_call" | custom-call | flops 1073741824 | bytes 7340032 | tf_op jit(solution)/shard_map/mine_a/pallas_call | solution.py:101
  14.1 0.0 copy-start
  14.1 0.0 copy-start.1
  14.1 0.0 collective-permute-done.1.there
  14.1 0.0 collective-permute-done.other
  14.1 0.8 copy-done
  14.9 0.2 copy-done.1
  15.1 5.0 %mine_b.1.rest_0_ = f32[8,65,8,128]{3,2,1,0:T(8,128)} custom-call(s32[1]{0:T(128)} %bitcast.5.index, bf16[8,2,256,1024]{3,2,1,0:T(8,128)(2,1)} %constant.36.clone.table, bf16[32,128,1024]{2,1,0:T(8,128)(2,1)} %traces.7, f32[4,8,16,8,128]{4,3,2,1,0:T(8,128)} %collective-permute-done.other, f32[8,128]{1,0:T(8,128)S(1)} %pad.4.here, ...), custom_call_target="tpu_custom_call" | custom-call | flops 1073741824 | bytes 7340032 | tf_op jit(solution)/shard_map/mine_b/pallas_call | solution.py:101
  20.1 5.6 %all-to-all-start = ((f32[8,65,8,128]{3,2,1,0:T(8,128)}), f32[8,65,8,128]{3,2,1,0:T(8,128)S(1)}, u32[]{:S(2)}, u32[]{:S(2)}) async-start(f32[8,65,8,128]{3,2,1,0:T(8,128)} %mine_b.1.rest_0_), calls=%async_computation | async-start | bytes 4259840 | tf_op jit(solution)/shard_map/all_to_all | solution.py:337
  25.7 0.5 collective-permute-start.3
  26.2 3.2 %collective-permute-start.4 = (f32[8,16,8,128]{3,2,1,0:T(8,128)}, f32[8,16,8,128]{3,2,1,0:T(8,128)S(1)}, u32[]{:S(2)}, u32[]{:S(2)}) collective-permute-start(f32[8,16,8,128]{3,2,1,0:T(8,128)} %copy-done), channel_id=1, source_target_pairs={{0,128},{8,136},{128,0},{136,8},{1,129},{9,137},{129,1},{137,9},{2... | collective-permute-start | bytes 1572872 | tf_op jit(solution)/shard_map/ppermute | solution.py:310
  29.4 0.0 copy-start.2
  29.4 1.1 %collective-permute-start.5 = (f32[8,16,8,128]{3,2,1,0:T(8,128)S(1)}, f32[8,16,8,128]{3,2,1,0:T(8,128)S(1)}, u32[]{:S(2)}, u32[]{:S(2)}) collective-permute-start(f32[8,16,8,128]{3,2,1,0:T(8,128)S(1)} %get-tuple-element.27), channel_id=1, source_target_pairs={{0,136},{8,128},{128,8},{136,0},{1,137},{9,129},{129,9},{137,1},{2... | collective-permute-start | bytes 1572872 | tf_op jit(solution)/shard_map/ppermute | solution.py:310
  30.4 10.4 %collective-permute-done.3.yl = f32[8,16,8,128]{3,2,1,0:T(8,128)S(1)} collective-permute-done((f32[8,16,8,128]{3,2,1,0:T(8,128)}, f32[8,16,8,128]{3,2,1,0:T(8,128)S(1)}, u32[]{:S(2)}, u32[]{:S(2)}) %collective-permute-start.3) | collective-permute-done | bytes 524320 | tf_op jit(solution)/shard_map/ppermute | solution.py:310
  40.8 11.4 %collective-permute-done.4.yh = f32[8,16,8,128]{3,2,1,0:T(8,128)S(1)} collective-permute-done((f32[8,16,8,128]{3,2,1,0:T(8,128)}, f32[8,16,8,128]{3,2,1,0:T(8,128)S(1)}, u32[]{:S(2)}, u32[]{:S(2)}) %collective-permute-start.4) | collective-permute-done | bytes 524320 | tf_op jit(solution)/shard_map/ppermute | solution.py:310
  52.2 2.4 %collective-permute-done.5.both = f32[8,16,8,128]{3,2,1,0:T(8,128)S(1)} collective-permute-done((f32[8,16,8,128]{3,2,1,0:T(8,128)S(1)}, f32[8,16,8,128]{3,2,1,0:T(8,128)S(1)}, u32[]{:S(2)}, u32[]{:S(2)}) %collective-permute-start.5) | collective-permute-done | bytes 524320 | tf_op jit(solution)/shard_map/ppermute | solution.py:310
  54.5 1.1 %sum_a.1.rest_0_ = f32[8,2,16,8,128]{4,3,2,1,0:T(8,128)} custom-call(f32[8,16,8,128]{3,2,1,0:T(8,128)S(1)} %get-tuple-element.24.rest_0_.own, f32[8,16,8,128]{3,2,1,0:T(8,128)S(1)} %collective-permute-done.3.yl, f32[8,16,8,128]{3,2,1,0:T(8,128)S(1)} %collective-permute-done.4.yh, f32[8,16,8,128]{3,2,1,0:T(8,128)S(1)} %collective-permute-done.5.both, ...), custom_call_target="tpu_custom_call" | custom-call | flops 262144 | bytes 3145728 | tf_op jit(solution)/shard_map/sum_a/pallas_call | solution.py:128
  55.7 0.0 all-to-all-done
  55.7 5.4 %all-to-all-start.1 = ((f32[8,2,16,8,128]{4,3,2,1,0:T(8,128)}), f32[8,2,16,8,128]{4,3,2,1,0:T(8,128)S(1)}, u32[]{:S(2)}, u32[]{:S(2)}) async-start(f32[8,2,16,8,128]{4,3,2,1,0:T(8,128)} %sum_a.1.rest_0_), calls=%async_computation.1 | async-start | bytes 2097152 | tf_op jit(solution)/shard_map/all_to_all | solution.py:339
  61.1 0.0 copy-done.2
  61.1 4.4 %slant_b.1 = (f32[4,128,128]{2,1,0:T(8,128)S(1)}, f32[4,128,128]{2,1,0:T(8,128)}, f32[4,128,128]{2,1,0:T(8,128)}, f32[4,128,128]{2,1,0:T(8,128)}, f32[8,128]{1,0:T(8,128)S(1)}) custom-call(s32[1]{0:T(128)} %bitcast.1.base, s32[1]{0:T(128)} %bitcast.2.yh, s32[1]{0:T(128)} %bitcast.3.yl, s32[1,128]{1,0:T(1,128)S(1)} %bitcast.14, f32[8,520,128]{2,1,0:T(8,128)S(1)} %bitcast.12, ...), custom_call_target="tpu_custom_call" | custom-call | flops 2147483648 | bytes 7340032 | tf_op jit(solution)/shard_map/slant_b/pallas_call | solution.py:259
  65.5 0.0 collective-permute-start.6
  65.5 2.5 %collective-permute-start.7 = (f32[4,128,128]{2,1,0:T(8,128)}, f32[4,128,128]{2,1,0:T(8,128)S(1)}, u32[]{:S(2)}, u32[]{:S(2)}) collective-permute-start(f32[4,128,128]{2,1,0:T(8,128)} %get-tuple-element.30), channel_id=1, source_target_pairs={{0,128},{8,136},{128,0},{136,8},{1,129},{9,137},{129,1},{137,9},{2... | collective-permute-start | bytes 786440 | tf_op jit(solution)/shard_map/ppermute | solution.py:310
  68.0 2.2 %collective-permute-start.8 = (f32[4,128,128]{2,1,0:T(8,128)}, f32[4,128,128]{2,1,0:T(8,128)S(1)}, u32[]{:S(2)}, u32[]{:S(2)}) collective-permute-start(f32[4,128,128]{2,1,0:T(8,128)} %get-tuple-element.31), channel_id=1, source_target_pairs={{0,136},{8,128},{128,8},{136,0},{1,137},{9,129},{129,9},{137,1},{2... | collective-permute-start | bytes 786440 | tf_op jit(solution)/shard_map/ppermute | solution.py:310
  70.2 1.7 %phase_a.1 = (bf16[4,256,512]{2,1,0:T(8,128)(2,1)S(1)}, bf16[4,256,512]{2,1,0:T(8,128)(2,1)S(1)}) custom-call(s32[1]{0:T(128)} %bitcast.1.base, s32[1]{0:T(128)} %bitcast.2.yh, s32[1]{0:T(128)} %bitcast.3.yl, s32[1,128]{1,0:T(1,128)S(1)} %bitcast.15, f32[8,128]{1,0:T(8,128)S(1)} %get-tuple-element.32.places), custom_call_target="tpu_custom_call" | custom-call | flops 16777216 | bytes 2097152 | tf_op jit(solution)/shard_map/phase_a/pallas_call | solution.py:210
  71.9 0.0 copy-start.3
  71.9 1.0 %copy-done.3 = bf16[4,256,512]{2,1,0:T(8,128)(2,1)} copy-done((bf16[4,256,512]{2,1,0:T(8,128)(2,1)}, bf16[4,256,512]{2,1,0:T(8,128)(2,1)S(1)}, u32[]{:S(2)}) %copy-start.3) | copy-done | bytes 1048600
  72.9 0.5 all-to-all-done.1
  73.4 0.0 copy-start.4
  73.4 1.2 %copy-done.4 = bf16[4,256,512]{2,1,0:T(8,128)(2,1)S(1)} copy-done((bf16[4,256,512]{2,1,0:T(8,128)(2,1)S(1)}, bf16[4,256,512]{2,1,0:T(8,128)(2,1)}, u32[]{:S(2)}) %copy-start.4) | copy-done | bytes 1048600
  74.6 0.9 slant_a.1
  75.5 0.0 collective-permute-done.6.yl
  75.5 0.8 collective-permute-done.7.yh
  76.3 2.5 %collective-permute-done.8.both = f32[4,128,128]{2,1,0:T(8,128)S(1)} collective-permute-done((f32[4,128,128]{2,1,0:T(8,128)}, f32[4,128,128]{2,1,0:T(8,128)S(1)}, u32[]{:S(2)}, u32[]{:S(2)}) %collective-permute-start.8) | collective-permute-done | bytes 262176 | tf_op jit(solution)/shard_map/ppermute | solution.py:310
  78.8 0.1 sum_b.1
  78.9 4.6 %collective-permute-start.10 = (f32[2,128,128]{2,1,0:T(8,128)S(1)}, f32[2,128,128]{2,1,0:T(8,128)S(1)}, u32[]{:S(2)}, u32[]{:S(2)}) collective-permute-start(f32[2,128,128]{2,1,0:T(8,128)S(1)} %get-tuple-element.41), channel_id=1, source_target_pairs={{0,4},{2,6},{4,0},{6,2},{1,5},{3,7},{5,1},{7,3},{8,12},{10,14},{12... | collective-permute-start | bytes 393224 | tf_op jit(solution)/shard_map/ppermute | solution.py:319
  83.5 1.4 %collective-permute-start.11 = (f32[2,128,128]{2,1,0:T(8,128)S(1)}, f32[2,128,128]{2,1,0:T(8,128)S(1)}, u32[]{:S(2)}, u32[]{:S(2)}) collective-permute-start(f32[2,128,128]{2,1,0:T(8,128)S(1)} %get-tuple-element.42), channel_id=1, source_target_pairs={{0,6},{2,0},{4,2},{6,4},{1,7},{3,1},{5,3},{7,5},{8,14},{10,8},{12,... | collective-permute-start | bytes 393224 | tf_op jit(solution)/shard_map/ppermute | solution.py:319
  84.9 2.7 %collective-permute-start.9 = (f32[2,128,128]{2,1,0:T(8,128)S(1)}, f32[2,128,128]{2,1,0:T(8,128)S(1)}, u32[]{:S(2)}, u32[]{:S(2)}) collective-permute-start(f32[2,128,128]{2,1,0:T(8,128)S(1)} %get-tuple-element.40), channel_id=1, source_target_pairs={{0,2},{2,4},{4,6},{6,0},{1,3},{3,5},{5,7},{7,1},{8,10},{10,12},{12... | collective-permute-start | bytes 393224 | tf_op jit(solution)/shard_map/ppermute | solution.py:319
  87.6 3.0 %collective-permute-done.10.rest_1_ = f32[2,128,128]{2,1,0:T(8,128)S(1)} collective-permute-done((f32[2,128,128]{2,1,0:T(8,128)S(1)}, f32[2,128,128]{2,1,0:T(8,128)S(1)}, u32[]{:S(2)}, u32[]{:S(2)}) %collective-permute-start.10) | collective-permute-done | bytes 131104 | tf_op jit(solution)/shard_map/ppermute | solution.py:319
  90.6 2.2 %collective-permute-done.11.rest_2_ = f32[2,128,128]{2,1,0:T(8,128)S(1)} collective-permute-done((f32[2,128,128]{2,1,0:T(8,128)S(1)}, f32[2,128,128]{2,1,0:T(8,128)S(1)}, u32[]{:S(2)}, u32[]{:S(2)}) %collective-permute-start.11) | collective-permute-done | bytes 131104 | tf_op jit(solution)/shard_map/ppermute | solution.py:319
  92.8 0.0 collective-permute-done.9.rest_0_
  92.8 0.8 finish.1
  (4 shorter events, 0.0 us)
Async XLA Ops:
  4.2 4.1 %copy-start.5 = (s32[32]{0:T(128)S(1)}, s32[32]{0:T(128)}, u32[]{:S(2)}) copy-start(s32[32]{0:T(128)} %param.5) | copy-start | bytes 388
  4.2 6.0 %collective-permute-start.2 = (f32[4,8,16,8,128]{4,3,2,1,0:T(8,128)}, f32[4,8,16,8,128]{4,3,2,1,0:T(8,128)}, u32[]{:S(2)}, u32[]{:S(2)}) collective-permute-start(f32[4,8,16,8,128]{4,3,2,1,0:T(8,128)} %other_a.1.rest_0_), channel_id=1, source_target_pairs={{0,64},{64,0},{1,65},{65,1},{2,66},{66,2},{3,67},{67,3},{4,68},{68... | collective-permute-start | bytes 6291464 | tf_op jit(solution)/shard_map/ppermute | solution.py:310
  7.6 6.5 %collective-permute-start = (f32[4,8,16,8,128]{4,3,2,1,0:T(8,128)S(1)}, f32[4,8,16,8,128]{4,3,2,1,0:T(8,128)}, u32[]{:S(2)}, u32[]{:S(2)}) collective-permute-start(f32[4,8,16,8,128]{4,3,2,1,0:T(8,128)S(1)} %other_b.1.rest_0_), channel_id=1, source_target_pairs={{0,64},{64,0},{1,65},{65,1},{2,66},{66,2},{3,67},{67,3},{4,68},{68... | collective-permute-start | bytes 6291464 | tf_op jit(solution)/shard_map/ppermute | solution.py:310
  8.6 5.5 %collective-permute-start.1 = (f32[8,128]{1,0:T(8,128)S(1)}, f32[8,128]{1,0:T(8,128)S(1)}, u32[]{:S(2)}, u32[]{:S(2)}) collective-permute-start(f32[8,128]{1,0:T(8,128)S(1)} %pad.4.here), channel_id=1, source_target_pairs={{0,8},{8,0},{1,9},{9,1},{2,10},{10,2},{3,11},{11,3},{4,12},{12,4},... | collective-permute-start | bytes 12296 | tf_op jit(solution)/shard_map/ppermute | solution.py:310
  14.1 0.8 copy-start
  14.1 1.0 %copy-start.1 = (f32[8,16,8,128]{3,2,1,0:T(8,128)}, f32[8,16,8,128]{3,2,1,0:T(8,128)S(1)}, u32[]{:S(2)}) copy-start(f32[8,16,8,128]{3,2,1,0:T(8,128)S(1)} %get-tuple-element.25) | copy-start | bytes 1572868
  20.1 35.6 %all-to-all-start = ((f32[8,65,8,128]{3,2,1,0:T(8,128)}), f32[8,65,8,128]{3,2,1,0:T(8,128)S(1)}, u32[]{:S(2)}, u32[]{:S(2)}) async-start(f32[8,65,8,128]{3,2,1,0:T(8,128)} %mine_b.1.rest_0_), calls=%async_computation | async-start | bytes 4259840 | tf_op jit(solution)/shard_map/all_to_all | solution.py:337
  25.7 15.1 %collective-permute-start.3 = (f32[8,16,8,128]{3,2,1,0:T(8,128)}, f32[8,16,8,128]{3,2,1,0:T(8,128)S(1)}, u32[]{:S(2)}, u32[]{:S(2)}) collective-permute-start(f32[8,16,8,128]{3,2,1,0:T(8,128)} %copy-done.1), channel_id=1, source_target_pairs={{0,8},{8,0},{128,136},{136,128},{1,9},{9,1},{129,137},{137,129},{2... | collective-permute-start | bytes 1572872 | tf_op jit(solution)/shard_map/ppermute | solution.py:310
  26.2 26.0 %collective-permute-start.4 = (f32[8,16,8,128]{3,2,1,0:T(8,128)}, f32[8,16,8,128]{3,2,1,0:T(8,128)S(1)}, u32[]{:S(2)}, u32[]{:S(2)}) collective-permute-start(f32[8,16,8,128]{3,2,1,0:T(8,128)} %copy-done), channel_id=1, source_target_pairs={{0,128},{8,136},{128,0},{136,8},{1,129},{9,137},{129,1},{137,9},{2... | collective-permute-start | bytes 1572872 | tf_op jit(solution)/shard_map/ppermute | solution.py:310
  29.4 31.7 %copy-start.2 = (s32[128]{0:T(128)S(1)}, s32[128]{0:T(128)}, u32[]{:S(2)}) copy-start(s32[128]{0:T(128)} %param.6) | copy-start | bytes 1540
  29.4 25.2 %collective-permute-start.5 = (f32[8,16,8,128]{3,2,1,0:T(8,128)S(1)}, f32[8,16,8,128]{3,2,1,0:T(8,128)S(1)}, u32[]{:S(2)}, u32[]{:S(2)}) collective-permute-start(f32[8,16,8,128]{3,2,1,0:T(8,128)S(1)} %get-tuple-element.27), channel_id=1, source_target_pairs={{0,136},{8,128},{128,8},{136,0},{1,137},{9,129},{129,9},{137,1},{2... | collective-permute-start | bytes 1572872 | tf_op jit(solution)/shard_map/ppermute | solution.py:310
  55.7 17.7 %all-to-all-start.1 = ((f32[8,2,16,8,128]{4,3,2,1,0:T(8,128)}), f32[8,2,16,8,128]{4,3,2,1,0:T(8,128)S(1)}, u32[]{:S(2)}, u32[]{:S(2)}) async-start(f32[8,2,16,8,128]{4,3,2,1,0:T(8,128)} %sum_a.1.rest_0_), calls=%async_computation.1 | async-start | bytes 2097152 | tf_op jit(solution)/shard_map/all_to_all | solution.py:339
  65.5 10.0 %collective-permute-start.6 = (f32[4,128,128]{2,1,0:T(8,128)}, f32[4,128,128]{2,1,0:T(8,128)S(1)}, u32[]{:S(2)}, u32[]{:S(2)}) collective-permute-start(f32[4,128,128]{2,1,0:T(8,128)} %get-tuple-element.29), channel_id=1, source_target_pairs={{0,8},{8,0},{128,136},{136,128},{1,9},{9,1},{129,137},{137,129},{2... | collective-permute-start | bytes 786440 | tf_op jit(solution)/shard_map/ppermute | solution.py:310
  65.5 10.8 %collective-permute-start.7 = (f32[4,128,128]{2,1,0:T(8,128)}, f32[4,128,128]{2,1,0:T(8,128)S(1)}, u32[]{:S(2)}, u32[]{:S(2)}) collective-permute-start(f32[4,128,128]{2,1,0:T(8,128)} %get-tuple-element.30), channel_id=1, source_target_pairs={{0,128},{8,136},{128,0},{136,8},{1,129},{9,137},{129,1},{137,9},{2... | collective-permute-start | bytes 786440 | tf_op jit(solution)/shard_map/ppermute | solution.py:310
  68.0 10.8 %collective-permute-start.8 = (f32[4,128,128]{2,1,0:T(8,128)}, f32[4,128,128]{2,1,0:T(8,128)S(1)}, u32[]{:S(2)}, u32[]{:S(2)}) collective-permute-start(f32[4,128,128]{2,1,0:T(8,128)} %get-tuple-element.31), channel_id=1, source_target_pairs={{0,136},{8,128},{128,8},{136,0},{1,137},{9,129},{129,9},{137,1},{2... | collective-permute-start | bytes 786440 | tf_op jit(solution)/shard_map/ppermute | solution.py:310
  71.9 1.0 %copy-start.3 = (bf16[4,256,512]{2,1,0:T(8,128)(2,1)}, bf16[4,256,512]{2,1,0:T(8,128)(2,1)S(1)}, u32[]{:S(2)}) copy-start(bf16[4,256,512]{2,1,0:T(8,128)(2,1)S(1)} %get-tuple-element.34.low) | copy-start | bytes 3145732
  73.4 1.2 %copy-start.4 = (bf16[4,256,512]{2,1,0:T(8,128)(2,1)S(1)}, bf16[4,256,512]{2,1,0:T(8,128)(2,1)}, u32[]{:S(2)}) copy-start(bf16[4,256,512]{2,1,0:T(8,128)(2,1)} %copy-done.3) | copy-start | bytes 3145732
  78.9 11.7 %collective-permute-start.10 = (f32[2,128,128]{2,1,0:T(8,128)S(1)}, f32[2,128,128]{2,1,0:T(8,128)S(1)}, u32[]{:S(2)}, u32[]{:S(2)}) collective-permute-start(f32[2,128,128]{2,1,0:T(8,128)S(1)} %get-tuple-element.41), channel_id=1, source_target_pairs={{0,4},{2,6},{4,0},{6,2},{1,5},{3,7},{5,1},{7,3},{8,12},{10,14},{12... | collective-permute-start | bytes 393224 | tf_op jit(solution)/shard_map/ppermute | solution.py:319
  83.5 9.3 %collective-permute-start.11 = (f32[2,128,128]{2,1,0:T(8,128)S(1)}, f32[2,128,128]{2,1,0:T(8,128)S(1)}, u32[]{:S(2)}, u32[]{:S(2)}) collective-permute-start(f32[2,128,128]{2,1,0:T(8,128)S(1)} %get-tuple-element.42), channel_id=1, source_target_pairs={{0,6},{2,0},{4,2},{6,4},{1,7},{3,1},{5,3},{7,5},{8,14},{10,8},{12,... | collective-permute-start | bytes 393224 | tf_op jit(solution)/shard_map/ppermute | solution.py:319
  84.9 7.8 %collective-permute-start.9 = (f32[2,128,128]{2,1,0:T(8,128)S(1)}, f32[2,128,128]{2,1,0:T(8,128)S(1)}, u32[]{:S(2)}, u32[]{:S(2)}) collective-permute-start(f32[2,128,128]{2,1,0:T(8,128)S(1)} %get-tuple-element.40), channel_id=1, source_target_pairs={{0,2},{2,4},{4,6},{6,0},{1,3},{3,5},{5,7},{7,1},{8,10},{10,12},{12... | collective-permute-start | bytes 393224 | tf_op jit(solution)/shard_map/ppermute | solution.py:319

commit v6 on v5

--- a/solution.py
+++ b/solution.py
@@ -160,7 +160,7 @@
 def phase_tables(n_d, base, yh, yl, slowness, positions, column, slow, high, low):
     slow[...] = jnp.broadcast_to(slowness[...].astype(jnp.float32), (NP, 128)).T.astype(jnp.int32)
     first = base[0] + yh[0] * 128 + yl[0] * 8
-    rows = 32
+    rows = 64
 
     def step(i, _):
         row = pl.multiple_of(i * rows, rows)

time: 95.1 us -> 95.2 us (level)
  no operation moved by 1% of the time
where the time goes in v6:
time: 95.2 us; the launch traced here: 93.6 us
  waiting for transfers between devices  33.1 us (35%)
  starting transfers between devices  31.4 us (33%)
  Pallas kernels  25.4 us (27%)
  local copies, waits for them, and re-layouts  3.58 us (4%)
    ppermute x9, waiting for transfers between devices, swap(): return lax.ppermute(value, axes, [(i, i ^ mask) for i in range(size)])  27.5 us
    pallas_call x4, Pallas kernels, dft(): pl.pallas_call(functools.partial(body, len(after)), grid_spec=pltpu.Prefe...  16.3 us
    ppermute x9, starting transfers between devices, swap(): return lax.ppermute(value, axes, [(i, i ^ mask) for i in range(size)])  11.6 us
    ppermute x3, starting transfers between devices, exchange_z(): lax.ppermute(parts[e], 'zh', shift(e))  8.72 us
    all_to_all x1, starting transfers between devices, body(): data_b = lax.all_to_all(mine_b, ('x', 'zl'), 0, 0, tiled=True)  5.66 us
    all_to_all x1, starting transfers between devices, body(): data_a = lax.all_to_all(both_a, ('x', 'zl'), 0, 0, tiled=True)  5.42 us
    ppermute x3, waiting for transfers between devices, exchange_z(): lax.ppermute(parts[e], 'zh', shift(e))  5.14 us
    pallas_call x1, Pallas kernels, slant_b(): pl.pallas_call(functools.partial(slant_b_body, len(after)), in_specs=[SCA...  4.48 us
  transfers between devices with their start and end apart: 14, of which 8 were waited for; matrix products, arithmetic and copies ran while one was open for 0% of the time, Pallas kernels for 16%

profile of v6, /device:TPU:64, one launch (start us, length us, event | category | flops | bytes accessed | tf_op | source)
XLA Modules:
  0.0 93.6 jit_solution(2717345271835534465)
XLA Ops:
  0.0 4.2 %other_a.1.rest_0_ = f32[4,8,16,8,128]{4,3,2,1,0:T(8,128)} custom-call(s32[1]{0:T(128)} %bitcast.5.index, bf16[8,2,256,1024]{3,2,1,0:T(8,128)(2,1)} %constant.36.clone.table, bf16[32,128,1024]{2,1,0:T(8,128)(2,1)} %traces.7), custom_call_target="tpu_custom_call" | custom-call | flops 1073741824 | bytes 7340032 | tf_op jit(solution)/shard_map/other_a/pallas_call | solution.py:101
  4.2 0.0 copy-start.5
  4.2 0.0 collective-permute-start.2
  4.2 3.3 %other_b.1.rest_0_ = f32[4,8,16,8,128]{4,3,2,1,0:T(8,128)S(1)} custom-call(s32[1]{0:T(128)} %bitcast.5.index, bf16[8,2,256,1024]{3,2,1,0:T(8,128)(2,1)} %constant.36.clone.table, bf16[32,128,1024]{2,1,0:T(8,128)(2,1)} %traces.7, f32[4,8,16,8,128]{4,3,2,1,0:T(8,128)} %other_a.1.rest_0_), custom_call_target="tpu_custom_call" | custom-call | flops 1073741824 | bytes 7340032 | tf_op jit(solution)/shard_map/other_b/pallas_call | solution.py:101
  7.6 0.6 collective-permute-start
  8.2 0.1 mul.45
  8.2 0.1 mul.46
  8.3 0.0 copy-done.5
  8.3 0.1 mul.41
  8.4 0.1 copy.6
  8.5 0.1 mul.43
  8.6 1.7 %collective-permute-start.1 = (f32[8,128]{1,0:T(8,128)S(1)}, f32[8,128]{1,0:T(8,128)S(1)}, u32[]{:S(2)}, u32[]{:S(2)}) collective-permute-start(f32[8,128]{1,0:T(8,128)S(1)} %pad.4.here), channel_id=1, source_target_pairs={{0,8},{8,0},{1,9},{9,1},{2,10},{10,2},{3,11},{11,3},{4,12},{12,4},... | collective-permute-start | bytes 12296 | tf_op jit(solution)/shard_map/ppermute | solution.py:310
  10.3 0.0 collective-permute-done.2.other
  10.3 3.8 %mine_a.1 = (f32[8,16,8,128]{3,2,1,0:T(8,128)S(1)}, f32[8,16,8,128]{3,2,1,0:T(8,128)S(1)}, f32[8,16,8,128]{3,2,1,0:T(8,128)S(1)}, f32[8,16,8,128]{3,2,1,0:T(8,128)S(1)}) custom-call(s32[1]{0:T(128)} %bitcast.5.index, bf16[8,2,256,1024]{3,2,1,0:T(8,128)(2,1)} %constant.36.clone.table, bf16[32,128,1024]{2,1,0:T(8,128)(2,1)} %traces.7, ...), custom_call_target="tpu_custom_call" | custom-call | flops 1073741824 | bytes 7340032 | tf_op jit(solution)/shard_map/mine_a/pallas_call | solution.py:101
  14.1 0.0 copy-start
  14.1 0.0 copy-start.1
  14.1 0.0 collective-permute-done.1.there
  14.1 0.0 collective-permute-done.other
  14.1 0.8 copy-done
  14.9 0.2 copy-done.1
  15.1 5.0 %mine_b.1.rest_0_ = f32[8,65,8,128]{3,2,1,0:T(8,128)} custom-call(s32[1]{0:T(128)} %bitcast.5.index, bf16[8,2,256,1024]{3,2,1,0:T(8,128)(2,1)} %constant.36.clone.table, bf16[32,128,1024]{2,1,0:T(8,128)(2,1)} %traces.7, f32[4,8,16,8,128]{4,3,2,1,0:T(8,128)} %collective-permute-done.other, f32[8,128]{1,0:T(8,128)S(1)} %pad.4.here, ...), custom_call_target="tpu_custom_call" | custom-call | flops 1073741824 | bytes 7340032 | tf_op jit(solution)/shard_map/mine_b/pallas_call | solution.py:101
  20.1 5.7 %all-to-all-start = ((f32[8,65,8,128]{3,2,1,0:T(8,128)}), f32[8,65,8,128]{3,2,1,0:T(8,128)S(1)}, u32[]{:S(2)}, u32[]{:S(2)}) async-start(f32[8,65,8,128]{3,2,1,0:T(8,128)} %mine_b.1.rest_0_), calls=%async_computation | async-start | bytes 4259840 | tf_op jit(solution)/shard_map/all_to_all | solution.py:337
  25.7 0.4 collective-permute-start.3
  26.2 3.2 %collective-permute-start.4 = (f32[8,16,8,128]{3,2,1,0:T(8,128)}, f32[8,16,8,128]{3,2,1,0:T(8,128)S(1)}, u32[]{:S(2)}, u32[]{:S(2)}) collective-permute-start(f32[8,16,8,128]{3,2,1,0:T(8,128)} %copy-done), channel_id=1, source_target_pairs={{0,128},{8,136},{128,0},{136,8},{1,129},{9,137},{129,1},{137,9},{2... | collective-permute-start | bytes 1572872 | tf_op jit(solution)/shard_map/ppermute | solution.py:310
  29.4 0.0 copy-start.2
  29.4 1.1 %collective-permute-start.5 = (f32[8,16,8,128]{3,2,1,0:T(8,128)S(1)}, f32[8,16,8,128]{3,2,1,0:T(8,128)S(1)}, u32[]{:S(2)}, u32[]{:S(2)}) collective-permute-start(f32[8,16,8,128]{3,2,1,0:T(8,128)S(1)} %get-tuple-element.27), channel_id=1, source_target_pairs={{0,136},{8,128},{128,8},{136,0},{1,137},{9,129},{129,9},{137,1},{2... | collective-permute-start | bytes 1572872 | tf_op jit(solution)/shard_map/ppermute | solution.py:310
  30.4 10.4 %collective-permute-done.3.yl = f32[8,16,8,128]{3,2,1,0:T(8,128)S(1)} collective-permute-done((f32[8,16,8,128]{3,2,1,0:T(8,128)}, f32[8,16,8,128]{3,2,1,0:T(8,128)S(1)}, u32[]{:S(2)}, u32[]{:S(2)}) %collective-permute-start.3) | collective-permute-done | bytes 524320 | tf_op jit(solution)/shard_map/ppermute | solution.py:310
  40.8 11.4 %collective-permute-done.4.yh = f32[8,16,8,128]{3,2,1,0:T(8,128)S(1)} collective-permute-done((f32[8,16,8,128]{3,2,1,0:T(8,128)}, f32[8,16,8,128]{3,2,1,0:T(8,128)S(1)}, u32[]{:S(2)}, u32[]{:S(2)}) %collective-permute-start.4) | collective-permute-done | bytes 524320 | tf_op jit(solution)/shard_map/ppermute | solution.py:310
  52.2 2.4 %collective-permute-done.5.both = f32[8,16,8,128]{3,2,1,0:T(8,128)S(1)} collective-permute-done((f32[8,16,8,128]{3,2,1,0:T(8,128)S(1)}, f32[8,16,8,128]{3,2,1,0:T(8,128)S(1)}, u32[]{:S(2)}, u32[]{:S(2)}) %collective-permute-start.5) | collective-permute-done | bytes 524320 | tf_op jit(solution)/shard_map/ppermute | solution.py:310
  54.5 1.1 %sum_a.1.rest_0_ = f32[8,2,16,8,128]{4,3,2,1,0:T(8,128)} custom-call(f32[8,16,8,128]{3,2,1,0:T(8,128)S(1)} %get-tuple-element.24.rest_0_.own, f32[8,16,8,128]{3,2,1,0:T(8,128)S(1)} %collective-permute-done.3.yl, f32[8,16,8,128]{3,2,1,0:T(8,128)S(1)} %collective-permute-done.4.yh, f32[8,16,8,128]{3,2,1,0:T(8,128)S(1)} %collective-permute-done.5.both, ...), custom_call_target="tpu_custom_call" | custom-call | flops 262144 | bytes 3145728 | tf_op jit(solution)/shard_map/sum_a/pallas_call | solution.py:128
  55.7 0.0 all-to-all-done
  55.7 5.4 %all-to-all-start.1 = ((f32[8,2,16,8,128]{4,3,2,1,0:T(8,128)}), f32[8,2,16,8,128]{4,3,2,1,0:T(8,128)S(1)}, u32[]{:S(2)}, u32[]{:S(2)}) async-start(f32[8,2,16,8,128]{4,3,2,1,0:T(8,128)} %sum_a.1.rest_0_), calls=%async_computation.1 | async-start | bytes 2097152 | tf_op jit(solution)/shard_map/all_to_all | solution.py:339
  61.1 0.0 copy-done.2
  61.1 4.5 %slant_b.1 = (f32[4,128,128]{2,1,0:T(8,128)S(1)}, f32[4,128,128]{2,1,0:T(8,128)}, f32[4,128,128]{2,1,0:T(8,128)}, f32[4,128,128]{2,1,0:T(8,128)}, f32[8,128]{1,0:T(8,128)S(1)}) custom-call(s32[1]{0:T(128)} %bitcast.1.base, s32[1]{0:T(128)} %bitcast.2.yh, s32[1]{0:T(128)} %bitcast.3.yl, s32[1,128]{1,0:T(1,128)S(1)} %bitcast.14, f32[8,520,128]{2,1,0:T(8,128)S(1)} %bitcast.12, ...), custom_call_target="tpu_custom_call" | custom-call | flops 2147483648 | bytes 7340032 | tf_op jit(solution)/shard_map/slant_b/pallas_call | solution.py:259
  65.6 0.0 collective-permute-start.6
  65.6 2.5 %collective-permute-start.7 = (f32[4,128,128]{2,1,0:T(8,128)}, f32[4,128,128]{2,1,0:T(8,128)S(1)}, u32[]{:S(2)}, u32[]{:S(2)}) collective-permute-start(f32[4,128,128]{2,1,0:T(8,128)} %get-tuple-element.30), channel_id=1, source_target_pairs={{0,128},{8,136},{128,0},{136,8},{1,129},{9,137},{129,1},{137,9},{2... | collective-permute-start | bytes 786440 | tf_op jit(solution)/shard_map/ppermute | solution.py:310
  68.1 2.2 %collective-permute-start.8 = (f32[4,128,128]{2,1,0:T(8,128)}, f32[4,128,128]{2,1,0:T(8,128)S(1)}, u32[]{:S(2)}, u32[]{:S(2)}) collective-permute-start(f32[4,128,128]{2,1,0:T(8,128)} %get-tuple-element.31), channel_id=1, source_target_pairs={{0,136},{8,128},{128,8},{136,0},{1,137},{9,129},{129,9},{137,1},{2... | collective-permute-start | bytes 786440 | tf_op jit(solution)/shard_map/ppermute | solution.py:310
  70.3 1.7 %phase_a.1 = (bf16[4,256,512]{2,1,0:T(8,128)(2,1)S(1)}, bf16[4,256,512]{2,1,0:T(8,128)(2,1)S(1)}) custom-call(s32[1]{0:T(128)} %bitcast.1.base, s32[1]{0:T(128)} %bitcast.2.yh, s32[1]{0:T(128)} %bitcast.3.yl, s32[1,128]{1,0:T(1,128)S(1)} %bitcast.15, f32[8,128]{1,0:T(8,128)S(1)} %get-tuple-element.32.places), custom_call_target="tpu_custom_call" | custom-call | flops 16777216 | bytes 2097152 | tf_op jit(solution)/shard_map/phase_a/pallas_call | solution.py:210
  72.0 0.0 copy-start.3
  72.0 1.0 %copy-done.3 = bf16[4,256,512]{2,1,0:T(8,128)(2,1)} copy-done((bf16[4,256,512]{2,1,0:T(8,128)(2,1)}, bf16[4,256,512]{2,1,0:T(8,128)(2,1)S(1)}, u32[]{:S(2)}) %copy-start.3) | copy-done | bytes 1048600
  73.0 0.4 all-to-all-done.1
  73.4 0.0 copy-start.4
  73.4 1.2 %copy-done.4 = bf16[4,256,512]{2,1,0:T(8,128)(2,1)S(1)} copy-done((bf16[4,256,512]{2,1,0:T(8,128)(2,1)S(1)}, bf16[4,256,512]{2,1,0:T(8,128)(2,1)}, u32[]{:S(2)}) %copy-start.4) | copy-done | bytes 1048600
  74.6 0.9 slant_a.1
  75.5 0.0 collective-permute-done.6.yl
  75.5 0.9 collective-permute-done.7.yh
  76.4 2.5 %collective-permute-done.8.both = f32[4,128,128]{2,1,0:T(8,128)S(1)} collective-permute-done((f32[4,128,128]{2,1,0:T(8,128)}, f32[4,128,128]{2,1,0:T(8,128)S(1)}, u32[]{:S(2)}, u32[]{:S(2)}) %collective-permute-start.8) | collective-permute-done | bytes 262176 | tf_op jit(solution)/shard_map/ppermute | solution.py:310
  78.9 0.1 sum_b.1
  79.0 4.6 %collective-permute-start.10 = (f32[2,128,128]{2,1,0:T(8,128)S(1)}, f32[2,128,128]{2,1,0:T(8,128)S(1)}, u32[]{:S(2)}, u32[]{:S(2)}) collective-permute-start(f32[2,128,128]{2,1,0:T(8,128)S(1)} %get-tuple-element.41), channel_id=1, source_target_pairs={{0,4},{2,6},{4,0},{6,2},{1,5},{3,7},{5,1},{7,3},{8,12},{10,14},{12... | collective-permute-start | bytes 393224 | tf_op jit(solution)/shard_map/ppermute | solution.py:319
  83.6 1.5 %collective-permute-start.11 = (f32[2,128,128]{2,1,0:T(8,128)S(1)}, f32[2,128,128]{2,1,0:T(8,128)S(1)}, u32[]{:S(2)}, u32[]{:S(2)}) collective-permute-start(f32[2,128,128]{2,1,0:T(8,128)S(1)} %get-tuple-element.42), channel_id=1, source_target_pairs={{0,6},{2,0},{4,2},{6,4},{1,7},{3,1},{5,3},{7,5},{8,14},{10,8},{12,... | collective-permute-start | bytes 393224 | tf_op jit(solution)/shard_map/ppermute | solution.py:319
  85.0 2.7 %collective-permute-start.9 = (f32[2,128,128]{2,1,0:T(8,128)S(1)}, f32[2,128,128]{2,1,0:T(8,128)S(1)}, u32[]{:S(2)}, u32[]{:S(2)}) collective-permute-start(f32[2,128,128]{2,1,0:T(8,128)S(1)} %get-tuple-element.40), channel_id=1, source_target_pairs={{0,2},{2,4},{4,6},{6,0},{1,3},{3,5},{5,7},{7,1},{8,10},{10,12},{12... | collective-permute-start | bytes 393224 | tf_op jit(solution)/shard_map/ppermute | solution.py:319
  87.7 3.0 %collective-permute-done.10.rest_1_ = f32[2,128,128]{2,1,0:T(8,128)S(1)} collective-permute-done((f32[2,128,128]{2,1,0:T(8,128)S(1)}, f32[2,128,128]{2,1,0:T(8,128)S(1)}, u32[]{:S(2)}, u32[]{:S(2)}) %collective-permute-start.10) | collective-permute-done | bytes 131104 | tf_op jit(solution)/shard_map/ppermute | solution.py:319
  90.7 2.2 %collective-permute-done.11.rest_2_ = f32[2,128,128]{2,1,0:T(8,128)S(1)} collective-permute-done((f32[2,128,128]{2,1,0:T(8,128)S(1)}, f32[2,128,128]{2,1,0:T(8,128)S(1)}, u32[]{:S(2)}, u32[]{:S(2)}) %collective-permute-start.11) | collective-permute-done | bytes 131104 | tf_op jit(solution)/shard_map/ppermute | solution.py:319
  92.9 0.0 collective-permute-done.9.rest_0_
  92.9 0.8 finish.1
  (4 shorter events, 0.0 us)
Async XLA Ops:
  4.2 4.1 %copy-start.5 = (s32[32]{0:T(128)S(1)}, s32[32]{0:T(128)}, u32[]{:S(2)}) copy-start(s32[32]{0:T(128)} %param.5) | copy-start | bytes 388
  4.2 6.0 %collective-permute-start.2 = (f32[4,8,16,8,128]{4,3,2,1,0:T(8,128)}, f32[4,8,16,8,128]{4,3,2,1,0:T(8,128)}, u32[]{:S(2)}, u32[]{:S(2)}) collective-permute-start(f32[4,8,16,8,128]{4,3,2,1,0:T(8,128)} %other_a.1.rest_0_), channel_id=1, source_target_pairs={{0,64},{64,0},{1,65},{65,1},{2,66},{66,2},{3,67},{67,3},{4,68},{68... | collective-permute-start | bytes 6291464 | tf_op jit(solution)/shard_map/ppermute | solution.py:310
  7.6 6.5 %collective-permute-start = (f32[4,8,16,8,128]{4,3,2,1,0:T(8,128)S(1)}, f32[4,8,16,8,128]{4,3,2,1,0:T(8,128)}, u32[]{:S(2)}, u32[]{:S(2)}) collective-permute-start(f32[4,8,16,8,128]{4,3,2,1,0:T(8,128)S(1)} %other_b.1.rest_0_), channel_id=1, source_target_pairs={{0,64},{64,0},{1,65},{65,1},{2,66},{66,2},{3,67},{67,3},{4,68},{68... | collective-permute-start | bytes 6291464 | tf_op jit(solution)/shard_map/ppermute | solution.py:310
  8.6 5.5 %collective-permute-start.1 = (f32[8,128]{1,0:T(8,128)S(1)}, f32[8,128]{1,0:T(8,128)S(1)}, u32[]{:S(2)}, u32[]{:S(2)}) collective-permute-start(f32[8,128]{1,0:T(8,128)S(1)} %pad.4.here), channel_id=1, source_target_pairs={{0,8},{8,0},{1,9},{9,1},{2,10},{10,2},{3,11},{11,3},{4,12},{12,4},... | collective-permute-start | bytes 12296 | tf_op jit(solution)/shard_map/ppermute | solution.py:310
  14.1 0.8 copy-start
  14.1 1.0 %copy-start.1 = (f32[8,16,8,128]{3,2,1,0:T(8,128)}, f32[8,16,8,128]{3,2,1,0:T(8,128)S(1)}, u32[]{:S(2)}) copy-start(f32[8,16,8,128]{3,2,1,0:T(8,128)S(1)} %get-tuple-element.25) | copy-start | bytes 1572868
  20.1 35.6 %all-to-all-start = ((f32[8,65,8,128]{3,2,1,0:T(8,128)}), f32[8,65,8,128]{3,2,1,0:T(8,128)S(1)}, u32[]{:S(2)}, u32[]{:S(2)}) async-start(f32[8,65,8,128]{3,2,1,0:T(8,128)} %mine_b.1.rest_0_), calls=%async_computation | async-start | bytes 4259840 | tf_op jit(solution)/shard_map/all_to_all | solution.py:337
  25.7 15.1 %collective-permute-start.3 = (f32[8,16,8,128]{3,2,1,0:T(8,128)}, f32[8,16,8,128]{3,2,1,0:T(8,128)S(1)}, u32[]{:S(2)}, u32[]{:S(2)}) collective-permute-start(f32[8,16,8,128]{3,2,1,0:T(8,128)} %copy-done.1), channel_id=1, source_target_pairs={{0,8},{8,0},{128,136},{136,128},{1,9},{9,1},{129,137},{137,129},{2... | collective-permute-start | bytes 1572872 | tf_op jit(solution)/shard_map/ppermute | solution.py:310
  26.2 26.0 %collective-permute-start.4 = (f32[8,16,8,128]{3,2,1,0:T(8,128)}, f32[8,16,8,128]{3,2,1,0:T(8,128)S(1)}, u32[]{:S(2)}, u32[]{:S(2)}) collective-permute-start(f32[8,16,8,128]{3,2,1,0:T(8,128)} %copy-done), channel_id=1, source_target_pairs={{0,128},{8,136},{128,0},{136,8},{1,129},{9,137},{129,1},{137,9},{2... | collective-permute-start | bytes 1572872 | tf_op jit(solution)/shard_map/ppermute | solution.py:310
  29.4 31.7 %copy-start.2 = (s32[128]{0:T(128)S(1)}, s32[128]{0:T(128)}, u32[]{:S(2)}) copy-start(s32[128]{0:T(128)} %param.6) | copy-start | bytes 1540
  29.4 25.2 %collective-permute-start.5 = (f32[8,16,8,128]{3,2,1,0:T(8,128)S(1)}, f32[8,16,8,128]{3,2,1,0:T(8,128)S(1)}, u32[]{:S(2)}, u32[]{:S(2)}) collective-permute-start(f32[8,16,8,128]{3,2,1,0:T(8,128)S(1)} %get-tuple-element.27), channel_id=1, source_target_pairs={{0,136},{8,128},{128,8},{136,0},{1,137},{9,129},{129,9},{137,1},{2... | collective-permute-start | bytes 1572872 | tf_op jit(solution)/shard_map/ppermute | solution.py:310
  55.7 17.7 %all-to-all-start.1 = ((f32[8,2,16,8,128]{4,3,2,1,0:T(8,128)}), f32[8,2,16,8,128]{4,3,2,1,0:T(8,128)S(1)}, u32[]{:S(2)}, u32[]{:S(2)}) async-start(f32[8,2,16,8,128]{4,3,2,1,0:T(8,128)} %sum_a.1.rest_0_), calls=%async_computation.1 | async-start | bytes 2097152 | tf_op jit(solution)/shard_map/all_to_all | solution.py:339
  65.6 9.9 %collective-permute-start.6 = (f32[4,128,128]{2,1,0:T(8,128)}, f32[4,128,128]{2,1,0:T(8,128)S(1)}, u32[]{:S(2)}, u32[]{:S(2)}) collective-permute-start(f32[4,128,128]{2,1,0:T(8,128)} %get-tuple-element.29), channel_id=1, source_target_pairs={{0,8},{8,0},{128,136},{136,128},{1,9},{9,1},{129,137},{137,129},{2... | collective-permute-start | bytes 786440 | tf_op jit(solution)/shard_map/ppermute | solution.py:310
  65.6 10.8 %collective-permute-start.7 = (f32[4,128,128]{2,1,0:T(8,128)}, f32[4,128,128]{2,1,0:T(8,128)S(1)}, u32[]{:S(2)}, u32[]{:S(2)}) collective-permute-start(f32[4,128,128]{2,1,0:T(8,128)} %get-tuple-element.30), channel_id=1, source_target_pairs={{0,128},{8,136},{128,0},{136,8},{1,129},{9,137},{129,1},{137,9},{2... | collective-permute-start | bytes 786440 | tf_op jit(solution)/shard_map/ppermute | solution.py:310
  68.1 10.8 %collective-permute-start.8 = (f32[4,128,128]{2,1,0:T(8,128)}, f32[4,128,128]{2,1,0:T(8,128)S(1)}, u32[]{:S(2)}, u32[]{:S(2)}) collective-permute-start(f32[4,128,128]{2,1,0:T(8,128)} %get-tuple-element.31), channel_id=1, source_target_pairs={{0,136},{8,128},{128,8},{136,0},{1,137},{9,129},{129,9},{137,1},{2... | collective-permute-start | bytes 786440 | tf_op jit(solution)/shard_map/ppermute | solution.py:310
  72.0 1.0 %copy-start.3 = (bf16[4,256,512]{2,1,0:T(8,128)(2,1)}, bf16[4,256,512]{2,1,0:T(8,128)(2,1)S(1)}, u32[]{:S(2)}) copy-start(bf16[4,256,512]{2,1,0:T(8,128)(2,1)S(1)} %get-tuple-element.34.low) | copy-start | bytes 3145732
  73.4 1.2 %copy-start.4 = (bf16[4,256,512]{2,1,0:T(8,128)(2,1)S(1)}, bf16[4,256,512]{2,1,0:T(8,128)(2,1)}, u32[]{:S(2)}) copy-start(bf16[4,256,512]{2,1,0:T(8,128)(2,1)} %copy-done.3) | copy-start | bytes 3145732
  79.0 11.7 %collective-permute-start.10 = (f32[2,128,128]{2,1,0:T(8,128)S(1)}, f32[2,128,128]{2,1,0:T(8,128)S(1)}, u32[]{:S(2)}, u32[]{:S(2)}) collective-permute-start(f32[2,128,128]{2,1,0:T(8,128)S(1)} %get-tuple-element.41), channel_id=1, source_target_pairs={{0,4},{2,6},{4,0},{6,2},{1,5},{3,7},{5,1},{7,3},{8,12},{10,14},{12... | collective-permute-start | bytes 393224 | tf_op jit(solution)/shard_map/ppermute | solution.py:319
  83.6 9.3 %collective-permute-start.11 = (f32[2,128,128]{2,1,0:T(8,128)S(1)}, f32[2,128,128]{2,1,0:T(8,128)S(1)}, u32[]{:S(2)}, u32[]{:S(2)}) collective-permute-start(f32[2,128,128]{2,1,0:T(8,128)S(1)} %get-tuple-element.42), channel_id=1, source_target_pairs={{0,6},{2,0},{4,2},{6,4},{1,7},{3,1},{5,3},{7,5},{8,14},{10,8},{12,... | collective-permute-start | bytes 393224 | tf_op jit(solution)/shard_map/ppermute | solution.py:319
  85.0 7.8 %collective-permute-start.9 = (f32[2,128,128]{2,1,0:T(8,128)S(1)}, f32[2,128,128]{2,1,0:T(8,128)S(1)}, u32[]{:S(2)}, u32[]{:S(2)}) collective-permute-start(f32[2,128,128]{2,1,0:T(8,128)S(1)} %get-tuple-element.40), channel_id=1, source_target_pairs={{0,2},{2,4},{4,6},{6,0},{1,3},{3,5},{5,7},{7,1},{8,10},{10,12},{12... | collective-permute-start | bytes 393224 | tf_op jit(solution)/shard_map/ppermute | solution.py:319
